TPU v7x, 256 devices: a whole 4x4x8 slice. The times are simulated.
256 devices in a mesh: grp: 8 (over x, y_hi), vocab: 32 (over y_lo, z, core).
Axes of the slice: x: 4, y: 4 (y_hi: 2, y_lo: 2; y = y_hi * 2 + y_lo), z: 8, core: 2. Of those that a mesh axis runs over, the one named last changes fastest.
Arguments:
- hidden: bfloat16 [1024, 4096], P('grp'), may hold values from -360 to 360
- weight: bfloat16 [4096, 75968], P('grp', 'vocab'), may hold values from -0.09375 to 0.09375
- teacher_panels: bfloat16 [512, 151936], P('grp', 'vocab'), may hold values from -20 to 172
- token_ids: int32 [1024], P('grp'), may hold values from 0 to 75967
- row_counts: int32 [8], P('grp'), may hold values from 64 to 128, as said below
Outputs:
- row_kl: float32 [1024], P('grp')
- hidden_grad: bfloat16 [1024, 4096], P('grp', 'vocab')
- weight_grad: bfloat16 [4096, 75968], P('grp', 'vocab')
Inputs may be any that keep to these rules, and one draw needn't show every extreme that they name: `row_counts`: one group's count is exactly 128.
All inputs are finite; a program needn't handle non-finite values.
Results may differ from a plain program's by a relative error of at most 0.005.
Values may be sent and summed in bfloat16 or wider, within the bound.
A program may use at most 128 MiB of HBM per device.

v0:
```python
import jax
import jax.numpy as jnp
from jax import lax
from jax.sharding import PartitionSpec as P

KL_SCALE = 256


def swapped(block, axis, stride):
    count = lax.axis_size(axis)
    route = []
    for low in range(count):
        high = low | 1 << stride
        if high != low and high < count:
            route += [(low, high), (high, low)]
    return lax.ppermute(block, axis, route)


def shards(hidden, weight, teacher_panels, token_ids, row_counts):
    tok_rows = hidden.shape[0]
    slab = weight.shape[1]
    vocab_pos = lax.axis_index("vocab")
    parity = vocab_pos % 2
    kept = lax.dynamic_slice_in_dim(teacher_panels, parity * slab, slab, 1)
    outgoing = lax.dynamic_slice_in_dim(teacher_panels, (1 - parity) * slab, slab, 1)
    incoming = swapped(outgoing, "vocab", 0)
    teacher = jnp.where(
        parity == 0, jnp.concatenate([kept, incoming], 0), jnp.concatenate([incoming, kept], 0)
    ).astype(jnp.float32)
    columns = lax.all_to_all(hidden, "grp", split_axis=1, concat_axis=0, tiled=True)
    block = columns
    logits = lax.psum_scatter(
        jnp.dot(block, weight, preferred_element_type=jnp.float32),
        "grp",
        scatter_dimension=0,
        tiled=True,
    )
    vocab_ids = vocab_pos * slab + lax.broadcasted_iota(jnp.int32, (1, slab), 1)
    chosen = (token_ids[:, None] == vocab_ids).astype(jnp.float32)
    pick_student = jnp.sum(chosen * logits, axis=1)
    pick_teacher = jnp.sum(chosen * teacher, axis=1)
    local_peak_s = jnp.max(logits, axis=1)
    local_peak_t = jnp.max(teacher, axis=1)
    peak_s, peak_t = lax.pmax((local_peak_s, local_peak_t), "vocab")
    student_exp = jnp.exp(logits - peak_s[:, None])
    teacher_exp = jnp.exp(teacher - peak_t[:, None])
    total_s, total_t, pick_student, pick_teacher = lax.psum(
        (jnp.sum(student_exp, axis=1), jnp.sum(teacher_exp, axis=1), pick_student, pick_teacher),
        "vocab",
    )
    student_norm = peak_s + jnp.log(total_s)
    teacher_norm = peak_t + jnp.log(total_t)
    probs = student_exp / total_s[:, None]
    log_ratio = logits - student_norm[:, None] - (teacher - teacher_norm[:, None])
    divergence = lax.psum(jnp.sum(probs * log_ratio, axis=1), "vocab")
    total_rows = lax.psum(jnp.sum(row_counts.astype(jnp.float32)), "grp")
    valid = lax.broadcasted_iota(jnp.int32, (tok_rows,), 0) < row_counts[0]
    row_weight = jnp.where(valid, tok_rows / total_rows, jnp.zeros_like(total_rows))
    advantage = pick_teacher - teacher_norm - (pick_student - student_norm)
    grad_logits = (
        row_weight[:, None]
        * (
            KL_SCALE * probs * (log_ratio - divergence[:, None])
            - advantage[:, None] * (chosen - probs)
        )
    ).astype(jnp.bfloat16)
    row_kl = jnp.where(valid, divergence, jnp.zeros_like(divergence))
    piece = lax.all_gather(grad_logits, "grp", axis=0, tiled=True)
    block = columns
    head_part = lax.dot_general(
        block, piece, (((0,), (0,)), ((), ())), preferred_element_type=jnp.float32
    )
    rows_part = lax.dot_general(
        piece, weight, (((1,), (1,)), ((), ())), preferred_element_type=jnp.float32
    )
    full_grad = lax.all_to_all(rows_part, "grp", split_axis=0, concat_axis=1, tiled=True)
    hidden_grad = lax.psum_scatter(full_grad, "vocab", scatter_dimension=1, tiled=True).astype(
        jnp.bfloat16
    )
    return (row_kl, hidden_grad, head_part.astype(jnp.bfloat16))


def solution(mesh):
    return jax.shard_map(
        shards,
        mesh=mesh,
        in_specs=(P("grp", None), P("grp", "vocab"), P("grp", "vocab"), P("grp"), P("grp")),
        out_specs=(P("grp"), P("grp", "vocab"), P("grp", "vocab")),
        check_vma=False,
    )
```

profile of v0, /device:TPU:6, one launch (start us, length us, event | category | flops | bytes accessed | tf_op | source)
XLA Modules:
  0.0 591.2 jit_solution(18321017880593445070)
XLA Ops:
  7.2 0.0 copy-start
  7.2 0.0 reduce-scatter.3.cloned.1.call-start
  7.2 2.4 copy.19
  9.6 22.2 %all_to_all.38 = bf16[128,8,512]{0,2,1:T(8,128)(2,1)S(1)} all-to-all(bf16[128,8,512]{0,2,1:T(8,128)(2,1)} %bitcast.22), channel_id=1, replica_groups=mesh['grp'=8,'vocab'=32] {'grp'}, dimensions={1} | all-to-all | bytes 2097152 | tf_op jit(solution)/shard_map/all_to_all | solution.py:30
  31.9 1.3 copy.20
  33.2 0.0 copy-done
  33.2 6.4 %fusion.14 = f32[1024,2374]{0,1:T(8,128)} fusion(bf16[1024,512]{1,0:T(8,128)(2,1)} %bitcast.24, bf16[512,2374]{0,1:T(8,128)(2,1)S(1)} %copy-done), kind=kOutput, calls=%fused_computation.31 | convolution fusion | flops 2489319424 | bytes 13203456 | tf_op jit(solution)/shard_map/dot_general | solution.py:33
  39.6 0.0 copy-start.2
  39.6 0.0 reduce-scatter.3.cloned.1.call-update
  39.6 0.0 all-gather.2.cloned.1.call-start
  39.7 1.0 copy-done.2
  40.7 0.9 constant_dynamic-slice_fusion
  41.6 0.0 collective-permute-start
  42.3 20.3 %psum.45 = f32[]{:T(128)} all-reduce(f32[]{:T(128)} %bitcast.4), channel_id=1, replica_groups=mesh['grp'=8,'vocab'=32] {'grp'}, use_global_device_ids=true, to_apply=%region_11.12 | all-reduce | flops 1 | bytes 8 | tf_op jit(solution)/shard_map/psum | solution.py:56
  62.6 1.1 copy.25
  64.4 0.0 collective-permute-done
  64.4 1.1 copy.22
  65.5 2.4 fusion.13
  67.9 105.4 %reduce-scatter.3.cloned.1.call-done = f32[128,2374]{0,1:T(8,128)} async-done(((f32[1024,2374]{0,1:T(8,128)}), f32[128,2374]{0,1:T(8,128)}) %reduce-scatter.3.cloned.1.call-update) | async-done | bytes 1215504 | tf_op jit(solution)/shard_map/reduce_scatter | solution.py:32
  173.2 1.6 reduce_max.23
  174.9 0.0 copy-start.3
  174.9 56.3 %all-reduce.2 = (f32[128]{0:T(128)S(1)}, f32[128]{0:T(128)S(1)}) all-reduce(bf16[128]{0:T(256)(128)(2,1)S(1)} %get-tuple-element.13, f32[128]{0:T(128)S(1)} %reduce_max.23), channel_id=1, replica_groups=mesh['grp'=8,'vocab'=32] {'vocab'}, use_global_device_ids=true, to_apply=%region_6.7 | all-reduce | flops 256 | bytes 1792 | tf_op jit(solution)/shard_map/pmax | solution.py:44
  231.1 1.7 fusion.2
  232.8 53.0 %all-reduce.1 = (f32[128]{0:T(128)S(1)}, f32[128]{0:T(128)S(1)}) all-reduce(f32[128]{0:T(128)S(1)} %get-tuple-element.17, f32[128]{0:T(128)S(1)} %get-tuple-element.18), channel_id=1, replica_groups=mesh['grp'=8,'vocab'=32] {'vocab'}, use_global_device_ids=true, to_apply=%region_8.9 | all-reduce | flops 256 | bytes 2048 | tf_op jit(solution)/shard_map/psum | solution.py:47
  285.8 0.0 copy-done.3
  285.8 2.2 fusion.5
  288.0 53.0 %all-reduce = (f32[128]{0:T(128)S(1)}, f32[128]{0:T(128)S(1)}, f32[128]{0:T(128)S(1)}) all-reduce(f32[128]{0:T(128)S(1)} %get-tuple-element.4, f32[128]{0:T(128)S(1)} %get-tuple-element.3, f32[128]{0:T(128)S(1)} %get-tuple-element.5), channel_id=1, replica_groups=mesh['grp'=8,'vocab'=32] {'vocab'}, use_global_device_ids=true, to_apply=%region_10.11 | all-reduce | flops 384 | bytes 3072 | tf_op jit(solution)/shard_map/psum | solution.py:55
  341.0 2.9 fusion.10
  343.9 0.0 all-gather.2.cloned.1.call-update
  343.9 0.0 reduce-scatter.5.cloned.1.call-start
  344.0 85.3 %all-gather.2.cloned.1.call-done = bf16[1024,2374]{0,1:T(8,128)(2,1)} async-done(((bf16[128,2374]{0,1:T(8,128)(2,1)}), bf16[1024,2374]{0,1:T(8,128)(2,1)}) %all-gather.2.cloned.1.call-update) | async-done | bytes 4861968 | tf_op jit(solution)/shard_map/all_gather | solution.py:68
  429.3 4.8 fusion.15
  434.1 29.4 %all_to_all.39 = f32[8,128,512]{2,1,0:T(8,128)S(1)} all-to-all(f32[8,128,512]{2,1,0:T(8,128)S(1)} %bitcast.23), channel_id=1, replica_groups=mesh['grp'=8,'vocab'=32] {'grp'}, dimensions={0} | all-to-all | bytes 4194304 | tf_op jit(solution)/shard_map/all_to_all | solution.py:76
  463.5 1.6 copy.26
  465.1 0.0 copy-start.1
  465.1 0.0 reduce-scatter.5.cloned.1.call-update
  465.1 0.5 compare_select_fusion.3
  465.6 0.7 copy-done.1
  466.3 6.3 %fusion = bf16[512,2374]{0,1:T(8,128)(2,1)} fusion(bf16[1024,2374]{0,1:T(8,128)(2,1)} %all-gather.2.cloned.1.call-done, bf16[1024,512]{1,0:T(8,128)(2,1)S(1)} %bitcast.25), kind=kOutput, calls=%fused_computation.1 | convolution fusion | flops 2490534912 | bytes 8341504 | tf_op jit(solution)/shard_map/dot_general | solution.py:70
  472.6 110.6 %reduce-scatter.5.cloned.1.call-done = f32[128,128]{1,0:T(8,128)} async-done(((f32[128,4096]{1,0:T(8,128)}), f32[128,128]{1,0:T(8,128)}) %reduce-scatter.5.cloned.1.call-update) | async-done | bytes 65552 | tf_op jit(solution)/shard_map/reduce_scatter | solution.py:77
  583.2 1.5 convert_element_type.25
  (5 shorter events, 0.0 us)
Async XLA Ops:
  7.2 26.0 %copy-start = (bf16[512,2374]{0,1:T(8,128)(2,1)S(1)}, bf16[512,2374]{0,1:T(8,128)(2,1)}, u32[]{:S(2)}) copy-start(bf16[512,2374]{0,1:T(8,128)(2,1)} %param.6) | copy-start | bytes 7292932
  7.2 166.1 %reduce-scatter.3.cloned.1.call-start = ((), (), s32[]{:S(2)}) async-start(), calls=%async_computation.4 | async-start | bytes 10948608 | tf_op jit(solution)/shard_map/reduce_scatter | solution.py:32
  39.6 1.1 copy-start.2
  39.6 389.7 %all-gather.2.cloned.1.call-start = ((), (), s32[]{:S(2)}) async-start(), calls=%async_computation.5 | async-start | bytes 5474304 | tf_op jit(solution)/shard_map/all_gather | solution.py:68
  41.6 22.8 %collective-permute-start = (bf16[64,2374]{1,0:T(8,128)(2,1)}, bf16[64,2374]{1,0:T(8,128)(2,1)S(1)}, u32[]{:S(2)}, u32[]{:S(2)}) collective-permute-start(bf16[64,2374]{1,0:T(8,128)(2,1)} %get-tuple-element.15), channel_id=1, source_target_pairs={{0,1},{1,0},{2,3},{3,2},{4,5},{5,4},{6,7},{7,6},{8,9},{9,8},{10,11... | collective-permute-start | bytes 911624 | tf_op jit(solution)/shard_map/ppermute | solution.py:16
  174.9 110.9 %copy-start.3 = (s32[128]{0:T(128)S(1)}, s32[128]{0:T(128)}, u32[]{:S(2)}) copy-start(s32[128]{0:T(128)} %param.8) | copy-start | bytes 1540
  343.9 239.3 %reduce-scatter.5.cloned.1.call-start = ((), (), s32[]{:S(2)}) async-start(), calls=%async_computation.6 | async-start | bytes 2162688 | tf_op jit(solution)/shard_map/reduce_scatter | solution.py:77
  465.1 1.2 copy-start.1
Sparse Core Ops, SparseCore 0:
  39.7 133.4 reduce-scatter.2
  344.1 85.1 all-gather.1
  465.2 117.9 reduce-scatter.4
where the time goes:
time: 592 us; the launch traced here: 591 us
  waiting for transfers between devices  301 us (51%)
  blocking collectives  234 us (40%)
  matrix products  17.5 us (3%)
  between operations  15.2 us (3%)
  other arithmetic  12.8 us (2%)
  local copies, waits for them, and re-layouts  10.1 us (2%)
    reduce_scatter x1, waiting for transfers between devices, shards(): lax.psum_scatter(full_grad, 'vocab', scatter_dimension=1, tiled=True)  111 us
    reduce_scatter x1, waiting for transfers between devices, shards(): lax.psum_scatter(jnp.dot(block, weight, preferred_element_type=jnp.float3...  105 us
    all_gather x1, waiting for transfers between devices, shards(): piece = lax.all_gather(grad_logits, 'grp', axis=0, tiled=True)  85.3 us
    pmax x1, blocking collectives, shards(): peak_s, peak_t = lax.pmax((local_peak_s, local_peak_t), 'vocab')  56.3 us
    psum x1, blocking collectives, shards(): divergence = lax.psum(jnp.sum(probs * log_ratio, axis=1), 'vocab')  53 us
    psum x1, blocking collectives, shards(): lax.psum((jnp.sum(student_exp, axis=1), jnp.sum(teacher_exp, axis=1), pic...  53 us
    all_to_all x1, blocking collectives, shards(): lax.all_to_all(rows_part, 'grp', split_axis=0, concat_axis=1, tiled=True)  29.4 us
    all_to_all x1, blocking collectives, shards(): lax.all_to_all(hidden, 'grp', split_axis=1, concat_axis=0, tiled=True)  22.2 us
  transfers between devices with their start and end apart: 4, of which 3 were waited for; matrix products, arithmetic and copies ran while one was open for 2% of the time, Pallas kernels for 0%

commit v1 on v0

v1 whole, which is shorter than its diff:
```python
import functools

import jax
import jax.numpy as jnp
from jax import lax
from jax.experimental import pallas as pl
from jax.experimental.pallas import tpu as pltpu
from jax.sharding import PartitionSpec as P

KL_SCALE = 256.0
MESH = pl.DeviceIdType.MESH
LOW = -1e30
NX, NH, NYL, NZ, NC = 4, 2, 2, 8, 2
TILE = 128
GROUP_PEERS = [(dx, dh) for dh in (1, 0) for dx in (1, 3, 2, 0) if dx or dh]
PAIR_PEERS = [(dx, dc) for dc in (0, 1) for dx in (1, 3, 2, 0) if dx or dc]
LINE_PEERS = [(dy, dz) for dy in (0, 1) for dz in range(NZ) if dy or dz]


def place():
    g = lax.axis_index("grp")
    v = lax.axis_index("vocab")
    return g // 2, g % 2, v // 16, (v // 2) % 8, v % 2


def device(x, h, yl, z, c):
    return {"grp": x * 2 + h, "vocab": yl * 16 + z * 2 + c}


def send(src, dst, ssem, rsem, target):
    copy = pltpu.make_async_remote_copy(
        src_ref=src, dst_ref=dst, send_sem=ssem, recv_sem=rsem, device_id=target, device_id_type=MESH
    )
    copy.start()
    return copy


def arrived(ref, sem):
    pltpu.make_async_copy(ref, ref, sem).wait()


def to_columns(tile):
    return jnp.transpose(jnp.concatenate([tile] * (TILE // 8), axis=0))


def merge(buf):
    peak_s = jnp.max(buf[:, :, 0], axis=0)
    scale_s = jnp.exp(buf[:, :, 0] - peak_s[None])
    peak_t = jnp.max(buf[:, :, 3], axis=0)
    scale_t = jnp.exp(buf[:, :, 3] - peak_t[None])
    return [
        peak_s,
        jnp.sum(buf[:, :, 1] * scale_s, axis=0),
        jnp.sum(buf[:, :, 2] * scale_s, axis=0),
        peak_t,
        jnp.sum(buf[:, :, 4] * scale_t, axis=0),
        jnp.sum(buf[:, :, 5], axis=0),
        jnp.sum(buf[:, :, 6], axis=0),
    ]


def loss_kernel(
    slab,
    chunks,
    hidden_ref,
    weight_ref,
    teacher_ref,
    meta_ref,
    grad_ref,
    own_ref,
    kl_ref,
    wide,
    heads,
    partial,
    landed,
    logits,
    teach,
    metas,
    near,
    far,
    outcome,
    cols,
    local_sem,
    hid_s,
    hid_r,
    fwd_s,
    fwd_r,
    core_s,
    core_r,
    meta_s,
    meta_r,
    w_s,
    w_r,
    half_s,
    half_r,
    t_s,
    t_r,
    near_s,
    near_r,
    far_s,
    far_r,
):
    x, h, yl, z, c = place()
    rows, depth = hidden_ref.shape[0], weight_ref.shape[0]
    half = NX * rows
    width = weight_ref.shape[1] // NX
    z_pair = z + 1 - 2 * lax.rem(z, 2)
    barrier = pltpu.get_barrier_semaphore()
    peers = [device((x + dx) % NX, (h + dh) % NH, yl, z, c) for dx, dh in GROUP_PEERS]
    peers += [device((x + dx) % NX, h, yl, z, 1 - c) for dx in range(NX)]
    peers += [device(x, h, (yl + dy) % NYL, (z + dz) % NZ, c) for dy, dz in LINE_PEERS]
    for peer in peers:
        pl.semaphore_signal(barrier, inc=1, device_id=peer, device_id_type=MESH)
    pl.semaphore_wait(barrier, len(peers))

    pending = []
    parity = lax.rem(z, 2)
    mine = 2 * c + parity

    def region(xs, hs, kx):
        return wide.at[
            pl.ds(pl.multiple_of(hs * half + xs * rows, rows), rows),
            pl.ds(pl.multiple_of(kx * depth, depth), depth),
        ]

    def block(kx, hs):
        return hidden_ref.at[:, pl.ds(pl.multiple_of((kx * 2 + hs) * depth, depth), depth)]

    for k, (dx, dh) in enumerate(GROUP_PEERS):
        xt, ht = (x + dx) % NX, (h + dh) % NH
        target = device(xt, ht, yl, z, c)
        pending.append(send(block(mine, ht), region(x, h, mine), hid_s.at[k], hid_r.at[k], target))
        pending.append(send(meta_ref, metas.at[x * 2 + h], meta_s.at[k], meta_r.at[k], target))
    for j, (low, size) in enumerate(chunks):
        for k, dx in enumerate((1, 3, 2)):
            xt = (x + dx) % NX
            pending.append(
                send(
                    weight_ref.at[:, pl.ds(pl.multiple_of(xt * width + low, TILE), size)],
                    heads.at[pl.ds(pl.multiple_of(x * depth, depth), depth), pl.ds(low, size)],
                    w_s.at[j * 3 + k],
                    w_r.at[j * 3 + k],
                    device(xt, h, yl, z, c),
                )
            )
    locals_ = []
    for kx in range(NX):
        locals_.append(pltpu.make_async_copy(block(kx, h), region(x, h, kx), local_sem.at[kx]))
    locals_.append(
        pltpu.make_async_copy(
            weight_ref.at[:, pl.ds(pl.multiple_of(x * width, TILE), width)],
            heads.at[pl.ds(pl.multiple_of(x * depth, depth), depth), :],
            local_sem.at[NX],
        )
    )
    locals_.append(
        pltpu.make_async_copy(
            teacher_ref.at[c, :, pl.ds(pl.multiple_of(x * width, TILE), width)],
            teach.at[pl.ds(pl.multiple_of(x * rows + c * (rows // 2), rows // 2), rows // 2), :],
            local_sem.at[NX + 1],
        )
    )
    for copy in locals_:
        copy.start()
    metas[x * 2 + h] = meta_ref[...]

    n = len(GROUP_PEERS)
    for k, (dx, dh) in enumerate(GROUP_PEERS):
        xs, hs = (x - dx + NX) % NX, (h + dh) % NH
        spot = region(xs, hs, mine)
        arrived(spot, hid_r.at[k])
        pending.append(send(spot, spot, fwd_s.at[k], fwd_r.at[k], device(x, h, yl, z_pair, c)))
        pending.append(send(spot, spot, core_s.at[k], core_r.at[k], device(x, h, yl, z, 1 - c)))
    for k, (dx, dh) in enumerate(GROUP_PEERS):
        xs, hs = (x - dx + NX) % NX, (h + dh) % NH
        spot = region(xs, hs, 2 * c + 1 - parity)
        arrived(spot, fwd_r.at[k])
        pending.append(send(spot, spot, core_s.at[n + k], core_r.at[n + k], device(x, h, yl, z, 1 - c)))
    for k, (dx, dh) in enumerate(GROUP_PEERS):
        xs, hs = (x - dx + NX) % NX, (h + dh) % NH
        arrived(region(xs, hs, 2 * (1 - c) + parity), core_r.at[k])
        arrived(region(xs, hs, 2 * (1 - c) + 1 - parity), core_r.at[n + k])
        arrived(metas.at[xs * 2 + hs], meta_r.at[k])
    for copy in locals_:
        copy.wait()

    def product(side, low, size):
        start = pl.multiple_of(side * half, half)
        return jnp.dot(
            wide[pl.ds(start, half), :], heads[:, low : low + size], preferred_element_type=jnp.float32
        )

    for j, (low, size) in enumerate(chunks):
        for k, dx in enumerate((1, 3, 2)):
            xs = (x - dx + NX) % NX
            arrived(
                heads.at[pl.ds(pl.multiple_of(xs * depth, depth), depth), pl.ds(low, size)],
                w_r.at[j * 3 + k],
            )
        if j == len(chunks) - 1:
            for k, (dx, dc) in enumerate(PAIR_PEERS):
                xt, ct = (x + dx) % NX, (c + dc) % NC
                pending.append(
                    send(
                        teacher_ref.at[ct, :, pl.ds(pl.multiple_of(xt * width, TILE), width)],
                        teach.at[pl.ds(pl.multiple_of(x * rows + c * (rows // 2), rows // 2), rows // 2), :],
                        t_s.at[k],
                        t_r.at[k],
                        device(xt, h, yl, z, ct),
                    )
                )
        partial[:, low : low + size] = product(1 - h, low, size)
        piece = pl.ds(low, size)
        pending.append(
            send(
                partial.at[:, piece], landed.at[:, piece], half_s.at[j], half_r.at[j],
                device(x, 1 - h, yl, z, c),
            )
        )
        logits[:, low : low + size] = product(h, low, size)
    own_ref[...] = wide[:, pl.ds(pl.multiple_of(x * depth, depth), depth)]
    for k, (dx, dc) in enumerate(PAIR_PEERS):
        xs, cs = (x - dx + NX) % NX, (c + dc) % NC
        arrived(
            teach.at[pl.ds(pl.multiple_of(xs * rows + cs * (rows // 2), rows // 2), rows // 2), :], t_r.at[k]
        )
    for j, (low, size) in enumerate(chunks):
        arrived(landed.at[:, pl.ds(low, size)], half_r.at[j])

    step = rows // 2
    lane = lax.broadcasted_iota(jnp.int32, (step, TILE), 1)
    column = lax.broadcasted_iota(jnp.int32, (step, width), 1)
    inside = column < slab - x * width
    base = ((yl * 16 + z * 2 + c) * slab + x * width).astype(jnp.float32)
    column_f = column.astype(jnp.float32)

    def fill(group, carry):
        cols[pl.ds(pl.multiple_of(group * rows, rows), rows), :] = to_columns(metas[group * 2 + h])
        return carry

    lax.fori_loop(0, NX, fill, 0)

    def measure(i, carry):
        span = pl.ds(pl.multiple_of(i * step, step), step)
        student = jnp.where(inside, logits[span, :] + landed[span, :], LOW)
        logits[span, :] = student
        raw = teach[span, :].astype(jnp.float32)
        teacher = jnp.where(inside, raw, LOW)
        chosen = (column_f == cols[span, :][:, 0:1] - base) & inside
        peak_s = jnp.max(student, axis=1, keepdims=True)
        peak_t = jnp.max(teacher, axis=1, keepdims=True)
        exp_s = jnp.exp(student - peak_s)
        exp_t = jnp.exp(teacher - peak_t)
        found = [
            peak_s,
            jnp.sum(exp_s, axis=1, keepdims=True),
            jnp.sum(exp_s * (student - raw), axis=1, keepdims=True),
            peak_t,
            jnp.sum(exp_t, axis=1, keepdims=True),
            jnp.sum(jnp.where(chosen, student, 0.0), axis=1, keepdims=True),
            jnp.sum(jnp.where(chosen, raw, 0.0), axis=1, keepdims=True),
        ]
        table = jnp.zeros((step, TILE), jnp.float32)
        for k, value in enumerate(found):
            table = jnp.where(lane == k + 1, value, table)
        cols[span, :] = jnp.where(lane == 0, cols[span, :], table)
        return carry

    lax.fori_loop(0, half // step, measure, 0)

    def pack(group, carry):
        table = jnp.transpose(cols[pl.ds(pl.multiple_of(group * rows, rows), rows), :])
        near[0, group] = table[0:8]
        return carry

    lax.fori_loop(0, NX, pack, 0)
    for k, (dx, dc) in enumerate(PAIR_PEERS):
        target = device((x + dx) % NX, h, yl, z, (c + dc) % NC)
        pending.append(send(near.at[0], near.at[k + 1], near_s.at[k], near_r.at[k], target))
    for k in range(len(PAIR_PEERS)):
        arrived(near.at[k + 1], near_r.at[k])

    merged = merge(near[:, :, 1:8])
    token_row = near[0, :, 0]
    for k, value in enumerate(merged):
        far[0, :, k] = value
    far[0, :, 7] = token_row
    for k, (dy, dz) in enumerate(LINE_PEERS):
        target = device(x, h, (yl + dy) % NYL, (z + dz) % NZ, c)
        pending.append(send(far.at[0], far.at[k + 1], far_s.at[k], far_r.at[k], target))
    for k in range(len(LINE_PEERS)):
        arrived(far.at[k + 1], far_r.at[k])
    peak_s, sum_s, weighted, peak_t, sum_t, pick_s, pick_t = merge(far[...])

    total_rows = jnp.sum(metas[:, 1, 0:1])
    student_norm = peak_s + jnp.log(sum_s)
    teacher_norm = peak_t + jnp.log(sum_t)
    mean_gap = weighted / sum_s
    divergence = mean_gap - student_norm + teacher_norm
    advantage = (pick_t - teacher_norm) - (pick_s - student_norm)
    counts = jnp.stack([metas[group * 2 + h][1] for group in range(NX)], axis=0)
    valid = lax.broadcasted_iota(jnp.int32, (NX, rows), 1).astype(jnp.float32) < counts
    row_weight = jnp.where(valid, rows / total_rows, 0.0)
    kl = jnp.where(valid, divergence, 0.0)
    own_group = lax.broadcasted_iota(jnp.int32, (NX, rows), 0) == x
    kl_ref[...] = jnp.sum(jnp.where(own_group, kl, 0.0), axis=0, keepdims=True)
    table = [
        peak_s, 1.0 / sum_s, mean_gap, row_weight * KL_SCALE, row_weight * advantage, token_row,
        token_row, token_row,
    ]
    for k, value in enumerate(table):
        outcome[:, k] = value

    def unpack(group, carry):
        cols[pl.ds(pl.multiple_of(group * rows, rows), rows), :] = to_columns(outcome[group])
        return carry

    lax.fori_loop(0, NX, unpack, 0)

    def finish(i, carry):
        span = pl.ds(pl.multiple_of(i * step, step), step)
        student = logits[span, :]
        raw = teach[span, :].astype(jnp.float32)
        table = cols[span, :]
        probs = jnp.exp(student - table[:, 0:1]) * table[:, 1:2]
        chosen = (column_f == table[:, 5:6] - base) & inside
        adv = table[:, 4:5]
        grad = probs * (table[:, 3:4] * ((student - raw) - table[:, 2:3]) + adv) - jnp.where(chosen, adv, 0.0)
        grad_ref[span, :] = grad.astype(jnp.bfloat16)
        return carry

    lax.fori_loop(0, half // step, finish, 0)
    for copy in pending:
        copy.wait_send()


def grads_kernel(
    grad_ref,
    own_ref,
    weight_ref,
    head_ref,
    hidden_ref,
    every,
    turned,
    rows_acc,
    paired,
    staged,
    lined,
    crossed,
    cross_out,
    final_out,
    final_in,
    local_sem,
    y_s,
    y_r,
    x_s,
    x_r,
    yx_s,
    yx_r,
    xy_s,
    xy_r,
    core_s,
    core_r,
    z_s,
    z_r,
    yl_s,
    yl_r,
    end_s,
    end_r,
):
    x, h, yl, z, c = place()
    half, width = grad_ref.shape
    tokens = 2 * half
    rows = half // NX
    split = 384
    g = x * 2 + h
    v = yl * 16 + z * 2 + c
    goal_g, goal_v = z, 4 * g + 2 * yl + c
    from_g, from_v = v // 4, ((v % 4) // 2) * 16 + g * 2 + v % 2
    moves = (goal_g != g) | (goal_v != v)
    partner = device(x, 1 - h, yl, z, c)
    mate = device(x, h, yl, z, 1 - c)
    across = device(x, h, 1 - yl, z, c)
    barrier = pltpu.get_barrier_semaphore()
    peers = [partner, mate, across]
    peers += [device((x + dx) % NX, h, yl, z, c) for dx in (1, 3, 2)]
    peers += [device(x, h, yl, (z + dz) % NZ, c) for dz in range(1, NZ)]
    for peer in peers:
        pl.semaphore_signal(barrier, inc=1, device_id=peer, device_id_type=MESH)

    @pl.when(moves)
    def _():
        pl.semaphore_signal(
            barrier, inc=1, device_id={"grp": from_g, "vocab": from_v}, device_id_type=MESH
        )

    pl.semaphore_wait(barrier, len(peers) + jnp.where(moves, 1, 0))

    def spot(xs, hs, low=0, size=width):
        return every.at[xs, pl.ds(pl.multiple_of(hs * half, half), half), pl.ds(low, size)]

    pending = [send(grad_ref, spot(x, h), y_s, y_r, partner)]
    for k, dx in enumerate((1, 3, 2)):
        pending.append(
            send(grad_ref, spot(x, h), x_s.at[k], x_r.at[k], device((x + dx) % NX, h, yl, z, c))
        )
    keep = pltpu.make_async_copy(grad_ref, spot(x, h), local_sem)
    keep.start()
    turned[...] = jnp.transpose(own_ref[...])
    rows_acc[...] = jnp.zeros_like(rows_acc)
    keep.wait()
    arrived(spot(x, 1 - h), y_r)
    for k, dx in enumerate((1, 3, 2)):
        tail = spot(x, 1 - h, split, width - split)
        pending.append(send(tail, tail, yx_s.at[k], yx_r.at[k], device((x + dx) % NX, h, yl, z, c)))

    def rows_part(xs):
        head = weight_ref[:, pl.ds(pl.multiple_of(xs * width, TILE), width)]

        def body(i, carry):
            span = pl.ds(pl.multiple_of(i * 256, 256), 256)
            out = lax.dot_general(
                every[xs, span, :], head, (((1,), (1,)), ((), ())), preferred_element_type=jnp.float32
            )
            for s in range(4):
                rows_acc[s, span, :] += out[:, s * TILE : (s + 1) * TILE]
            return carry

        lax.fori_loop(0, tokens // 256, body, 0)

    def head_part(xs):
        def body(i, carry):
            span = pl.ds(pl.multiple_of(i * 256, 256), 256)
            out = jnp.dot(turned[span, :], every[xs], preferred_element_type=jnp.float32)
            head_ref[span, pl.ds(pl.multiple_of(xs * width, TILE), width)] = out.astype(jnp.bfloat16)
            return carry

        lax.fori_loop(0, turned.shape[0] // 256, body, 0)

    rows_part(x)
    head_part(x)
    for k, dx in enumerate((1, 3, 2)):
        xs = (x - dx + NX) % NX
        arrived(spot(xs, h), x_r.at[k])
        lead = spot(xs, h, 0, split)
        pending.append(send(lead, lead, xy_s.at[k], xy_r.at[k], partner))
    for k, dx in enumerate((1, 3, 2)):
        xs = (x - dx + NX) % NX
        arrived(spot(xs, 1 - h, split, width - split), yx_r.at[k])
        arrived(spot(xs, 1 - h, 0, split), xy_r.at[k])
        rows_part(xs)
        if k < 2:
            head_part(xs)
    for b in range(NYL):
        pending.append(
            send(rows_acc.at[2 * b + 1 - c], paired.at[b], core_s.at[b], core_r.at[b], mate)
        )
    head_part((x - 2 + NX) % NX)
    for b in range(NYL):
        arrived(paired.at[b], core_r.at[b])

    def gather(t, carry):
        start = pl.multiple_of((t % 2) * half + (t // 2) * rows, rows)
        for b in range(NYL):
            staged[t, b] = rows_acc[2 * b + c, pl.ds(start, rows), :] + paired[b, pl.ds(start, rows), :]
        return carry

    lax.fori_loop(0, NZ, gather, 0)
    for dz in range(1, NZ):
        zt = (z + dz) % NZ
        pending.append(
            send(staged.at[zt], lined.at[dz], z_s.at[dz], z_r.at[dz], device(x, h, yl, zt, c))
        )
    for dz in range(1, NZ):
        arrived(lined.at[dz], z_r.at[dz])
    total = staged[z]
    for dz in range(1, NZ):
        total = total + lined[dz]
    lined[0] = total
    cross_out[...] = lined[0, 1 - yl]
    pending.append(send(cross_out, crossed, yl_s, yl_r, across))
    arrived(crossed, yl_r)
    final_out[...] = (lined[0, yl] + crossed[...]).astype(jnp.bfloat16)

    @pl.when(moves)
    def _():
        last = send(final_out, final_in, end_s, end_r, {"grp": goal_g, "vocab": goal_v})
        last.wait()
        hidden_ref[...] = final_in[...]

    @pl.when(jnp.logical_not(moves))
    def _():
        hidden_ref[...] = final_out[...]

    for copy in pending:
        copy.wait_send()


def dma(*shape):
    return pltpu.SemaphoreType.DMA(shape)


def shards(hidden, weight, teacher_panels, token_ids, row_counts):
    rows, model = hidden.shape
    depth, slab = weight.shape
    width = -(-slab // (NX * TILE)) * TILE
    extra = NX * width - slab
    half, tokens = NX * rows, NX * NH * rows
    padded = jnp.pad(weight, ((0, 0), (0, extra)))
    teacher = jnp.stack(
        [
            jnp.pad(teacher_panels[:, :slab], ((0, 0), (0, extra))),
            jnp.pad(teacher_panels[:, slab:], ((0, 0), (0, extra))),
        ]
    )
    meta = jnp.concatenate(
        [
            token_ids.astype(jnp.float32)[None],
            jnp.broadcast_to(row_counts.astype(jnp.float32)[:, None], (7, rows)),
        ]
    )
    chunks = []
    low = 0
    while low < width:
        chunks.append((low, min(256, width - low)))
        low += 256
    n, m, q = len(GROUP_PEERS), len(PAIR_PEERS), len(LINE_PEERS)
    vmem = pl.BlockSpec(memory_space=pltpu.VMEM)
    f32, bf16 = jnp.float32, jnp.bfloat16
    grad, own, kl = pl.pallas_call(
        functools.partial(loss_kernel, slab, tuple(chunks)),
        name="loss",
        out_shape=[
            jax.ShapeDtypeStruct((half, width), bf16),
            jax.ShapeDtypeStruct((tokens, depth), bf16),
            jax.ShapeDtypeStruct((1, rows), f32),
        ],
        in_specs=[vmem] * 4,
        out_specs=[vmem] * 3,
        scratch_shapes=[
            pltpu.VMEM((tokens, NX * depth), bf16),
            pltpu.VMEM((NX * depth, width), bf16),
            pltpu.VMEM((half, width), f32),
            pltpu.VMEM((half, width), f32),
            pltpu.VMEM((half, width), f32),
            pltpu.VMEM((half, width), bf16),
            pltpu.VMEM((NX * NH, 8, rows), f32),
            pltpu.VMEM((m + 1, NX, 8, rows), f32),
            pltpu.VMEM((q + 1, NX, 8, rows), f32),
            pltpu.VMEM((NX, 8, rows), f32),
            pltpu.VMEM((half, TILE), f32),
            dma(NX + 2),
            dma(n), dma(n), dma(n), dma(n), dma(2 * n), dma(2 * n), dma(n), dma(n),
            dma(3 * len(chunks)), dma(3 * len(chunks)), dma(len(chunks)), dma(len(chunks)),
            dma(m), dma(m), dma(m), dma(m), dma(q), dma(q),
        ],
        compiler_params=pltpu.CompilerParams(
            collective_id=1, has_side_effects=True, vmem_limit_bytes=56 * 2**20
        ),
    )(hidden, padded, teacher, meta)
    head_grad, hidden_grad = pl.pallas_call(
        grads_kernel,
        name="grads",
        out_shape=[
            jax.ShapeDtypeStruct((depth, NX * width), bf16),
            jax.ShapeDtypeStruct((rows, TILE), bf16),
        ],
        in_specs=[vmem] * 3,
        out_specs=[vmem] * 2,
        scratch_shapes=[
            pltpu.VMEM((NX, tokens, width), bf16),
            pltpu.VMEM((depth, tokens), bf16),
            pltpu.VMEM((4, tokens, TILE), f32),
            pltpu.VMEM((NYL, tokens, TILE), f32),
            pltpu.VMEM((NZ, NYL, rows, TILE), f32),
            pltpu.VMEM((NZ, NYL, rows, TILE), f32),
            pltpu.VMEM((rows, TILE), f32),
            pltpu.VMEM((rows, TILE), f32),
            pltpu.VMEM((rows, TILE), bf16),
            pltpu.VMEM((rows, TILE), bf16),
            pltpu.SemaphoreType.DMA,
            pltpu.SemaphoreType.DMA, pltpu.SemaphoreType.DMA,
            dma(3), dma(3), dma(3), dma(3), dma(3), dma(3),
            dma(NYL), dma(NYL), dma(NZ), dma(NZ),
            pltpu.SemaphoreType.DMA, pltpu.SemaphoreType.DMA,
            pltpu.SemaphoreType.DMA, pltpu.SemaphoreType.DMA,
        ],
        compiler_params=pltpu.CompilerParams(
            collective_id=2, has_side_effects=True, vmem_limit_bytes=56 * 2**20
        ),
    )(grad, own, padded)
    return kl[0], hidden_grad, head_grad[:, :slab]


def solution(mesh):
    return jax.shard_map(
        shards,
        mesh=mesh,
        in_specs=(P("grp", None), P("grp", "vocab"), P("grp", "vocab"), P("grp"), P("grp")),
        out_specs=(P("grp"), P("grp", "vocab"), P("grp", "vocab")),
        check_vma=False,
    )
```

time: 592 us -> 203 us (0.34)
  waiting for transfers between devices: 301 us -> 0 us
  blocking collectives: 234 us -> 0 us
  Pallas kernels: 0 us -> 187 us
  matrix products: 17.5 us -> 0 us
  between operations: 15.2 us -> 1.33 us
  other arithmetic: 12.8 us -> 2.6 us
    reduce_scatter x2 -> x0, waiting for transfers between devices: 216 us -> none  [the longest x1 111 us: shards(): lax.psum_scatter(full_grad, 'vocab', scatter_dimension=1, tiled=True)]
    pallas_call x0 -> x2, Pallas kernels: none -> 187 us  [the longest x1 93.7 us: shards(): pl.pallas_call(functools.partial(loss_kernel, slab, tuple(chunks)), name=...]
    psum x3 -> x0, blocking collectives: 126 us -> none  [the longest x1 53 us: shards(): divergence = lax.psum(jnp.sum(probs * log_ratio, axis=1), 'vocab')]
    all_gather x1 -> x0, waiting for transfers between devices: 85.3 us -> none  [shards(): piece = lax.all_gather(grad_logits, 'grp', axis=0, tiled=True)]
    pmax x1 -> x0, blocking collectives: 56.3 us -> none  [shards(): peak_s, peak_t = lax.pmax((local_peak_s, local_peak_t), 'vocab')]
    all_to_all x2 -> x0, blocking collectives: 51.6 us -> none  [the longest x1 29.4 us: shards(): lax.all_to_all(rows_part, 'grp', split_axis=0, concat_axis=1, tiled=True)]
    dot_general x3 -> x0, matrix products: 17.5 us -> none  [the longest x1 6.42 us: shards(): jnp.dot(block, weight, preferred_element_type=jnp.float32)]
  transfers between devices with their start and end apart: 4 -> 0, of which waited for: 3 -> 0; matrix products, arithmetic and copies ran while one was open for 2% -> 0% of each run, Pallas kernels for 0% -> 0%
where the time goes in v1:
time: 203 us
  Pallas kernels  187 us (92%)
  local copies, waits for them, and re-layouts  12.1 us (6%)
  other arithmetic  2.6 us (1%)
    pallas_call x1, Pallas kernels, shards(): pl.pallas_call(functools.partial(loss_kernel, slab, tuple(chunks)), name=...  93.7 us
    pallas_call x1, Pallas kernels, shards(): pl.pallas_call(grads_kernel, name='grads', out_shape=[jax.ShapeDtypeStruc...  93.2 us
    unnamed x8, local copies, waits for them, and re-layouts  6.79 us

profile of v1, /device:TPU:6, one launch (start us, length us, event | category | flops | bytes accessed | tf_op | source)
XLA Modules:
  0.0 202.9 jit_solution(2689762944662491101)
XLA Ops:
  1.3 0.7 convert_bitcast_fusion
  1.9 0.6 concatenate.3.meta_ref
  2.5 1.1 slice.11
  3.7 1.0 pad_bitcast_fusion
  4.7 0.9 pad_maximum_fusion.teacher_ref
  5.6 3.1 %copy.8 = bf16[512,2374]{1,0:T(8,128)(2,1)S(1)} copy(bf16[512,2374]{0,1:T(8,128)(2,1)} %param.6) | data formatting | bytes 4861952 | tf_op args[1]
  8.7 1.7 pad.12.weight_ref
  10.4 93.7 %loss.1 = (bf16[512,640]{1,0:T(8,128)(2,1)}, bf16[1024,512]{1,0:T(8,128)(2,1)}, f32[1,128]{1,0:T(1,128)}) custom-call(bf16[128,4096]{1,0:T(8,128)(2,1)} %hidden_ref.1, bf16[512,2560]{1,0:T(8,128)(2,1)} %pad.12.weight_ref, bf16[2,64,2560]{2,1,0:T(8,128)(2,1)} %pad_maximum_fusion.teacher_ref, f32[8,128]{1,0:T(8,128)} %concatenate.3.meta_ref), custom_call_target="tpu_custom_call" | custom-call | tf_op jit(solution)/shard_map/loss/pallas_call | solution.py:530
  104.2 93.2 %grads.1 = (bf16[512,2560]{1,0:T(8,128)(2,1)}, bf16[128,128]{1,0:T(8,128)(2,1)}) custom-call(bf16[512,640]{1,0:T(8,128)(2,1)} %get-tuple-element.9.grad_ref, bf16[1024,512]{1,0:T(8,128)(2,1)} %get-tuple-element.10.own_ref, bf16[512,2560]{1,0:T(8,128)(2,1)} %pad.12.weight_ref), custom_call_target="tpu_custom_call" | custom-call | tf_op jit(solution)/shard_map/grads/pallas_call | solution.py:561
  197.4 1.9 slice.12
  199.3 0.0 copy-start.1
  199.3 0.0 copy-start
  199.3 2.5 %copy.9 = bf16[512,2374]{0,1:T(8,128)(2,1)} copy(bf16[512,2374]{1,0:T(8,128)(2,1)S(1)} %slice.12) | data formatting | bytes 4861952
  201.8 0.0 copy-done.1
  201.8 0.5 copy.13
  202.3 0.0 copy-done
  202.3 0.6 copy.14
Async XLA Ops:
  199.3 2.5 %copy-start.1 = (f32[1,128]{1,0:T(1,128)S(1)}, f32[1,128]{1,0:T(1,128)}, u32[]{:S(2)}) copy-start(f32[1,128]{1,0:T(1,128)} %get-tuple-element.8) | copy-start | bytes 1540
  199.3 3.1 %copy-start = (bf16[128,128]{1,0:T(8,128)(2,1)S(1)}, bf16[128,128]{1,0:T(8,128)(2,1)}, u32[]{:S(2)}) copy-start(bf16[128,128]{1,0:T(8,128)(2,1)} %get-tuple-element.22) | copy-start | bytes 98308

commit v2 on v0

v2 whole, which is shorter than its diff:
```python
import functools

import jax
import jax.numpy as jnp
from jax import lax
from jax.experimental import pallas as pl
from jax.experimental.pallas import tpu as pltpu
from jax.sharding import PartitionSpec as P

KL_SCALE = 256.0
MESH = pl.DeviceIdType.MESH
LOW = -1e30
NX, NH, NYL, NZ, NC = 4, 2, 2, 8, 2
TILE = 128
GROUP_PEERS = [(dx, dh) for dh in (1, 0) for dx in (1, 3, 2, 0) if dx or dh]
PAIR_PEERS = [(dx, dc) for dc in (0, 1) for dx in (1, 3, 2, 0) if dx or dc]
LINE_PEERS = [(dy, dz) for dy in (0, 1) for dz in range(NZ) if dy or dz]


def place():
    g = lax.axis_index("grp")
    v = lax.axis_index("vocab")
    return g // 2, g % 2, v // 16, (v // 2) % 8, v % 2


def device(x, h, yl, z, c):
    return {"grp": x * 2 + h, "vocab": yl * 16 + z * 2 + c}


def to_columns(tile):
    return jnp.transpose(jnp.concatenate([tile] * (TILE // 8), axis=0))


def merge(buf):
    peak_s = jnp.max(buf[:, :, 0], axis=0)
    scale_s = jnp.exp(buf[:, :, 0] - peak_s[None])
    peak_t = jnp.max(buf[:, :, 3], axis=0)
    scale_t = jnp.exp(buf[:, :, 3] - peak_t[None])
    return [
        peak_s,
        jnp.sum(buf[:, :, 1] * scale_s, axis=0),
        jnp.sum(buf[:, :, 2] * scale_s, axis=0),
        peak_t,
        jnp.sum(buf[:, :, 4] * scale_t, axis=0),
        jnp.sum(buf[:, :, 5], axis=0),
        jnp.sum(buf[:, :, 6], axis=0),
    ]


def fused_kernel(
    slab,
    chunks,
    hidden_ref,
    weight_ref,
    panel_ref,
    token_ref,
    count_ref,
    head_ref,
    out_ref,
    kl_ref,
    padded,
    wide,
    heads,
    partial,
    landed,
    logits,
    teacher,
    teach,
    meta,
    metas,
    near,
    far,
    outcome,
    cols,
    every,
    rows_out,
    paired,
    staged,
    lined,
    cross_out,
    crossed,
    final_out,
    final_in,
    local_sem,
    sent,
    got,
    z_sent,
    z_got,
    end_sem,
):
    x, h, yl, z, c = place()
    rows, depth = hidden_ref.shape[0], padded.shape[1]
    above = GROUP_PEERS[:NX]
    beside = GROUP_PEERS[NX:]
    half = NX * rows
    width = padded.shape[0] // NX
    z_pair = z + 1 - 2 * lax.rem(z, 2)
    g = x * 2 + h
    v = yl * 16 + z * 2 + c
    goal_g, goal_v = z, 4 * g + 2 * yl + c
    from_g, from_v = v // 4, ((v % 4) // 2) * 16 + g * 2 + v % 2
    moves = (goal_g != g) | (goal_v != v)
    partner = device(x, 1 - h, yl, z, c)
    mate = device(x, h, yl, z, 1 - c)
    across = device(x, h, 1 - yl, z, c)
    right, left = (x + 1) % NX, (x + NX - 1) % NX
    opposite = (x + 2) % NX
    to_right, to_left = device(right, h, yl, z, c), device(left, h, yl, z, c)

    barrier = pltpu.get_barrier_semaphore()
    peers = [device((x + dx) % NX, (h + dh) % NH, yl, z, c) for dx, dh in GROUP_PEERS]
    peers += [device((x + dx) % NX, h, yl, z, 1 - c) for dx in range(NX)]
    peers += [device(x, h, (yl + dy) % NYL, (z + dz) % NZ, c) for dy, dz in LINE_PEERS]
    for peer in peers:
        pl.semaphore_signal(barrier, inc=1, device_id=peer, device_id_type=MESH)

    @pl.when(moves)
    def _():
        pl.semaphore_signal(
            barrier, inc=1, device_id={"grp": from_g, "vocab": from_v}, device_id_type=MESH
        )

    meta[...] = jnp.where(
        lax.broadcasted_iota(jnp.int32, meta.shape, 0) == 0,
        token_ref[...].astype(jnp.float32),
        count_ref[0].astype(jnp.float32),
    )
    metas[g] = meta[...]
    padded[0:slab, :] = weight_ref[...]
    padded[slab:, :] = jnp.zeros((NX * width - slab, depth), padded.dtype)
    pl.semaphore_wait(barrier, len(peers) + jnp.where(moves, 1, 0))

    pending = []

    def send(src, dst, target):
        slot = len(pending)
        copy = pltpu.make_async_remote_copy(
            src_ref=src, dst_ref=dst, send_sem=sent.at[slot], recv_sem=got.at[slot],
            device_id=target, device_id_type=MESH,
        )
        copy.start()
        pending.append(copy)
        return slot

    def arrived(ref, slot):
        pltpu.make_async_copy(ref, ref, got.at[slot]).wait()

    parity = lax.rem(z, 2)
    mine, other = 2 * c + parity, 2 * c + 1 - parity

    def region(xs, hs, kx):
        return wide.at[
            pl.ds(pl.multiple_of(hs * half + xs * rows, rows), rows),
            pl.ds(pl.multiple_of(kx * depth, depth), depth),
        ]

    def block(kx, hs):
        return hidden_ref.at[:, pl.ds(pl.multiple_of((kx * 2 + hs) * depth, depth), depth)]

    hid = {}

    def spread(peers):
        for dx, dh in peers:
            xt, ht = (x + dx) % NX, (h + dh) % NH
            hid[dx, dh] = send(block(mine, ht), region(x, h, mine), device(xt, ht, yl, z, c))

    def weight_rows(xs, low, size):
        return pl.ds(pl.multiple_of(xs * width + low, TILE), size)

    def head_spot(kx, low, size):
        return heads.at[pl.ds(low, size), pl.ds(pl.multiple_of(kx * depth, depth), depth)]

    wgt = []

    def spread_weight():
        if len(wgt) < len(chunks):
            low, size = chunks[len(wgt)]
            wgt.append(
                [
                    send(
                        padded.at[weight_rows((x + dx) % NX, low, size), :],
                        head_spot(x, low, size),
                        device((x + dx) % NX, h, yl, z, c),
                    )
                    for dx in (1, 3, 2)
                ]
            )

    fwd, near_core, far_core, met = {}, {}, {}, {}

    def source(peer):
        return (x - peer[0] + NX) % NX, (h + peer[1]) % NH

    def pass_on(peers):
        for peer in peers:
            spot = region(*source(peer), mine)
            arrived(spot, hid[peer])
            fwd[peer] = send(spot, spot, device(x, h, yl, z_pair, c))
            near_core[peer] = send(spot, spot, mate)

    def pass_core(peers):
        for peer in peers:
            spot = region(*source(peer), other)
            arrived(spot, fwd[peer])
            far_core[peer] = send(spot, spot, mate)

    def collect(peers):
        for peer in peers:
            xs, hs = source(peer)
            arrived(region(xs, hs, 2 * (1 - c) + parity), near_core[peer])
            arrived(region(xs, hs, 2 * (1 - c) + 1 - parity), far_core[peer])

    spread(above)
    spread_weight()
    for dx, dh in GROUP_PEERS:
        met[dx, dh] = send(meta, metas.at[g], device((x + dx) % NX, (h + dh) % NH, yl, z, c))
    locals_ = [
        pltpu.make_async_copy(block(kx, h), region(x, h, kx), local_sem.at[kx]) for kx in range(NX)
    ]
    locals_.append(
        pltpu.make_async_copy(
            padded.at[weight_rows(x, 0, width), :], head_spot(x, 0, width), local_sem.at[NX]
        )
    )
    for copy in locals_:
        copy.start()

    teacher[...] = jnp.zeros_like(teacher)
    for side in range(NC):
        teacher[side, :, 0:slab] = panel_ref[:, side * slab : (side + 1) * slab]

    pass_on(above)
    spread_weight()
    pass_core(above)
    spread_weight()
    spread(beside)
    for copy in locals_:
        copy.wait()
    for peer in GROUP_PEERS:
        xs, hs = source(peer)
        arrived(metas.at[xs * 2 + hs], met[peer])
    collect(above)

    def product(side, low, size):
        return lax.dot_general(
            wide[pl.ds(pl.multiple_of(side * half, half), half), :],
            heads[low : low + size, :],
            (((1,), (1,)), ((), ())),
            preferred_element_type=jnp.float32,
        )

    def teach_spot(xs, cs):
        step = rows // 2
        return teach.at[pl.ds(pl.multiple_of(xs * rows + cs * step, step), step), :]

    def teacher_piece(xt, ct):
        return teacher.at[ct, :, pl.ds(pl.multiple_of(xt * width, TILE), width)]

    halves, teaching = [], []
    for j, (low, size) in enumerate(chunks):
        for k, dx in enumerate((1, 3, 2)):
            arrived(head_spot((x - dx + NX) % NX, low, size), wgt[j][k])
        partial[:, low : low + size] = product(1 - h, low, size)
        piece = pl.ds(low, size)
        halves.append(send(partial.at[:, piece], landed.at[:, piece], partner))
        spread_weight()
        if j == 1:
            pass_on(beside)
        if j == 2:
            pass_core(beside)
        if j == len(chunks) - 2:
            keep = pltpu.make_async_copy(teacher_piece(x, c), teach_spot(x, c), local_sem.at[0])
            keep.start()
            for dx, dc in PAIR_PEERS:
                xt, ct = (x + dx) % NX, (c + dc) % NC
                teaching.append(send(teacher_piece(xt, ct), teach_spot(x, c), device(xt, h, yl, z, ct)))
    collect(beside)
    for low in range(0, width, 256):
        size = min(256, width - low)
        logits[:, low : low + size] = product(h, low, size)

    step = rows // 2
    lane = lax.broadcasted_iota(jnp.int32, (step, TILE), 1)
    column = lax.broadcasted_iota(jnp.int32, (step, width), 1)
    inside = column < slab - x * width
    base = (v * slab + x * width).astype(jnp.float32)
    column_f = column.astype(jnp.float32)

    def fill(group, carry):
        cols[pl.ds(pl.multiple_of(group * rows, rows), rows), :] = to_columns(metas[group * 2 + h])
        return carry

    lax.fori_loop(0, NX, fill, 0)
    keep.wait()
    for k, (dx, dc) in enumerate(PAIR_PEERS):
        arrived(teach_spot((x - dx + NX) % NX, (c + dc) % NC), teaching[k])

    def measure_teacher(i, carry):
        span = pl.ds(pl.multiple_of(i * step, step), step)
        raw = teach[span, :].astype(jnp.float32)
        masked = jnp.where(inside, raw, LOW)
        old = cols[span, :]
        chosen = (column_f == old[:, 0:1] - base) & inside
        peak = jnp.max(masked, axis=1, keepdims=True)
        total = jnp.sum(jnp.exp(masked - peak), axis=1, keepdims=True)
        pick = jnp.sum(jnp.where(chosen, raw, 0.0), axis=1, keepdims=True)
        table = jnp.where(lane == 4, peak, jnp.where(lane == 5, total, pick))
        cols[span, :] = jnp.where(lane == 0, old, table)
        return carry

    lax.fori_loop(0, half // step, measure_teacher, 0)
    for j, (low, size) in enumerate(chunks):
        arrived(landed.at[:, pl.ds(low, size)], halves[j])

    def measure_student(i, carry):
        span = pl.ds(pl.multiple_of(i * step, step), step)
        student = jnp.where(inside, logits[span, :] + landed[span, :], LOW)
        logits[span, :] = student
        raw = teach[span, :].astype(jnp.float32)
        old = cols[span, :]
        chosen = (column_f == old[:, 0:1] - base) & inside
        peak = jnp.max(student, axis=1, keepdims=True)
        exps = jnp.exp(student - peak)
        found = {
            1: peak,
            2: jnp.sum(exps, axis=1, keepdims=True),
            3: jnp.sum(exps * (student - raw), axis=1, keepdims=True),
            6: jnp.sum(jnp.where(chosen, student, 0.0), axis=1, keepdims=True),
        }
        for k, value in found.items():
            old = jnp.where(lane == k, value, old)
        cols[span, :] = old
        return carry

    lax.fori_loop(0, half // step, measure_student, 0)

    def pack(group, carry):
        table = jnp.transpose(cols[pl.ds(pl.multiple_of(group * rows, rows), rows), :])
        near[0, group] = table[0:8]
        return carry

    lax.fori_loop(0, NX, pack, 0)
    slots = [
        send(near.at[0], near.at[k + 1], device((x + dx) % NX, h, yl, z, (c + dc) % NC))
        for k, (dx, dc) in enumerate(PAIR_PEERS)
    ]
    for k, slot in enumerate(slots):
        arrived(near.at[k + 1], slot)
    for k, value in enumerate(merge(near[:, :, 1:8])):
        far[0, :, k] = value
    token_row = near[0, :, 0]
    far[0, :, 7] = token_row
    slots = [
        send(far.at[0], far.at[k + 1], device(x, h, (yl + dy) % NYL, (z + dz) % NZ, c))
        for k, (dy, dz) in enumerate(LINE_PEERS)
    ]
    for k, slot in enumerate(slots):
        arrived(far.at[k + 1], slot)
    peak_s, sum_s, weighted, peak_t, sum_t, pick_s, pick_t = merge(far[...])

    total_rows = jnp.sum(metas[:, 1, 0:1])
    student_norm = peak_s + jnp.log(sum_s)
    teacher_norm = peak_t + jnp.log(sum_t)
    mean_gap = weighted / sum_s
    divergence = mean_gap - student_norm + teacher_norm
    advantage = (pick_t - teacher_norm) - (pick_s - student_norm)
    counts = jnp.stack([metas[group * 2 + h][1] for group in range(NX)], axis=0)
    valid = lax.broadcasted_iota(jnp.int32, (NX, rows), 1).astype(jnp.float32) < counts
    row_weight = jnp.where(valid, rows / total_rows, 0.0)
    kl = jnp.where(valid, divergence, 0.0)
    own_group = lax.broadcasted_iota(jnp.int32, (NX, rows), 0) == x
    kl_ref[...] = jnp.sum(jnp.where(own_group, kl, 0.0), axis=0, keepdims=True)
    table = [
        peak_s, 1.0 / sum_s, mean_gap, row_weight * KL_SCALE, row_weight * advantage, token_row,
        token_row, token_row,
    ]
    for k, value in enumerate(table):
        outcome[:, k] = value

    def place_of(xs, hs, p, low=0, size=None):
        start = pl.multiple_of(hs * half + p * rows + low, step)
        return every.at[xs, pl.ds(start, rows if size is None else size), :]

    own_start = h * half

    def finish(i, carry):
        span = pl.ds(pl.multiple_of(i * step, step), step)
        student = logits[span, :]
        raw = teach[span, :].astype(jnp.float32)
        table = cols[span, :]
        probs = jnp.exp(student - table[:, 0:1]) * table[:, 1:2]
        chosen = (column_f == table[:, 5:6] - base) & inside
        adv = table[:, 4:5]
        grad = probs * (table[:, 3:4] * ((student - raw) - table[:, 2:3]) + adv)
        grad = grad - jnp.where(chosen, adv, 0.0)
        every[x, pl.ds(pl.multiple_of(own_start + i * step, step), step), :] = grad.astype(jnp.bfloat16)
        return carry

    direct = []

    def spread_grad():
        if len(direct) < NX:
            spot = place_of(x, h, len(direct))
            direct.append([send(spot, spot, to_right), send(spot, spot, to_left), send(spot, spot, partner)])

    per = rows // step
    for p in range(NX):
        cols[p * rows : (p + 1) * rows, :] = to_columns(outcome[p])
        lax.fori_loop(p * per, (p + 1) * per, finish, 0)
        if p < 2:
            spread_grad()

    def rows_part(p):
        for side in range(NH):
            start = side * half + p * rows
            out = jnp.zeros((rows, depth), jnp.float32)
            for xs in range(NX):
                out = out + jnp.dot(
                    every[xs, start : start + rows, :],
                    padded[xs * width : (xs + 1) * width, :],
                    preferred_element_type=jnp.float32,
                )
            for s in range(4):
                rows_out[p, s % 2, s // 2, side] = out[:, s * TILE : (s + 1) * TILE]
        return send(rows_out.at[p, 1 - c], paired.at[p], mate)

    def line_up(p, slot):
        arrived(paired.at[p], slot)
        for side in range(NH):
            t = 2 * p + side
            for b in range(NYL):
                staged[t, b] = rows_out[p, c, b, side] + paired[p, b, side]

            @pl.when(z != t)
            def _():
                pltpu.make_async_remote_copy(
                    src_ref=staged.at[t], dst_ref=lined.at[z], send_sem=z_sent.at[t],
                    recv_sem=z_got.at[z], device_id=device(x, h, yl, t, c), device_id_type=MESH,
                ).start()

    far_own, last, paired_slots = [], [], []
    for p in range(NX + 3):
        if p < NX:
            arrived(place_of(left, h, p), direct[p][0])
            lead = place_of(left, h, p, 0, step)
            a = send(lead, lead, to_right)
            arrived(place_of(right, h, p), direct[p][1])
            tail = place_of(right, h, p, step, step)
            far_own.append((a, send(tail, tail, to_left)))
            spot = place_of(x, 1 - h, p)
            arrived(spot, direct[p][2])
            last.append([send(spot, spot, to_right), send(spot, spot, to_left)])
            spread_grad()
        if 1 <= p <= NX:
            q = p - 1
            arrived(place_of(opposite, h, q, 0, step), far_own[q][0])
            arrived(place_of(opposite, h, q, step, step), far_own[q][1])
            spot = place_of(opposite, h, q)
            last[q].append(send(spot, spot, partner))
        if 2 <= p <= NX + 1:
            q = p - 2
            arrived(place_of(left, 1 - h, q), last[q][0])
            arrived(place_of(right, 1 - h, q), last[q][1])
            arrived(place_of(opposite, 1 - h, q), last[q][2])
            paired_slots.append(rows_part(q))
        if 3 <= p:
            line_up(p - 3, paired_slots[p - 3])

    for xs in range(NX):
        size = min(width, slab - xs * width)
        out = lax.dot_general(
            every[xs],
            wide[:, pl.ds(pl.multiple_of(x * depth, depth), depth)],
            (((0,), (0,)), ((), ())),
            preferred_element_type=jnp.float32,
        )
        head_ref[xs * width : xs * width + size, :] = out[:size].astype(jnp.bfloat16)
    lined[z] = staged[z]
    for s in range(NZ):

        @pl.when(z != s)
        def _():
            pltpu.make_async_copy(lined.at[s], lined.at[s], z_got.at[s]).wait()

    total = lined[0]
    for s in range(1, NZ):
        total = total + lined[s]
    staged[z] = total
    cross_out[...] = staged[z, 1 - yl]
    slot = send(cross_out, crossed, across)
    arrived(crossed, slot)
    final_out[...] = (staged[z, yl] + crossed[...]).astype(jnp.bfloat16)

    @pl.when(moves)
    def _():
        copy = pltpu.make_async_remote_copy(
            src_ref=final_out, dst_ref=final_in, send_sem=end_sem.at[0], recv_sem=end_sem.at[1],
            device_id={"grp": goal_g, "vocab": goal_v}, device_id_type=MESH,
        )
        copy.start()
        copy.wait()
        out_ref[...] = final_in[...]

    @pl.when(jnp.logical_not(moves))
    def _():
        out_ref[...] = final_out[...]

    for copy in pending:
        copy.wait_send()
    for t in range(NZ):

        @pl.when(z != t)
        def _():
            pltpu.make_async_copy(staged.at[t], staged.at[t], z_sent.at[t]).wait()


def shards(hidden, weight, teacher_panels, token_ids, row_counts):
    rows = hidden.shape[0]
    depth, slab = weight.shape
    width = -(-slab // (NX * TILE)) * TILE
    half, tokens = NX * rows, NX * NH * rows
    chunks = tuple((low, TILE) for low in range(0, width, TILE))
    m, q = len(PAIR_PEERS), len(LINE_PEERS)
    vmem = pl.BlockSpec(memory_space=pltpu.VMEM)
    f32, bf16 = jnp.float32, jnp.bfloat16
    copies = 5 * len(GROUP_PEERS) + 4 * len(chunks) + 2 * m + q + 9 * NX + 1
    head_grad, hidden_grad, kl = pl.pallas_call(
        functools.partial(fused_kernel, slab, chunks),
        name="distill",
        out_shape=[
            jax.ShapeDtypeStruct((slab, depth), bf16),
            jax.ShapeDtypeStruct((rows, TILE), bf16),
            jax.ShapeDtypeStruct((1, rows), f32),
        ],
        in_specs=[vmem] * 4 + [pl.BlockSpec(memory_space=pltpu.SMEM)],
        out_specs=[vmem] * 3,
        scratch_shapes=[
            pltpu.VMEM((NX * width, depth), bf16),
            pltpu.VMEM((tokens, NX * depth), bf16),
            pltpu.VMEM((width, NX * depth), bf16),
            pltpu.VMEM((half, width), f32),
            pltpu.VMEM((half, width), f32),
            pltpu.VMEM((half, width), f32),
            pltpu.VMEM((NC, rows // 2, NX * width), bf16),
            pltpu.VMEM((half, width), bf16),
            pltpu.VMEM((8, rows), f32),
            pltpu.VMEM((NX * NH, 8, rows), f32),
            pltpu.VMEM((m + 1, NX, 8, rows), f32),
            pltpu.VMEM((q + 1, NX, 8, rows), f32),
            pltpu.VMEM((NX, 8, rows), f32),
            pltpu.VMEM((half, TILE), f32),
            pltpu.VMEM((NX, tokens, width), bf16),
            pltpu.VMEM((NX, NC, NYL, NH, rows, TILE), f32),
            pltpu.VMEM((NX, NYL, NH, rows, TILE), f32),
            pltpu.VMEM((NZ, NYL, rows, TILE), f32),
            pltpu.VMEM((NZ, NYL, rows, TILE), f32),
            pltpu.VMEM((rows, TILE), f32),
            pltpu.VMEM((rows, TILE), f32),
            pltpu.VMEM((rows, TILE), bf16),
            pltpu.VMEM((rows, TILE), bf16),
            pltpu.SemaphoreType.DMA((NX + 1,)),
            pltpu.SemaphoreType.DMA((copies,)),
            pltpu.SemaphoreType.DMA((copies,)),
            pltpu.SemaphoreType.DMA((NZ,)),
            pltpu.SemaphoreType.DMA((NZ,)),
            pltpu.SemaphoreType.DMA((2,)),
        ],
        compiler_params=pltpu.CompilerParams(
            collective_id=1, has_side_effects=True, vmem_limit_bytes=56 * 2**20
        ),
    )(hidden, weight.T, teacher_panels, token_ids[None], row_counts)
    return kl[0], hidden_grad, head_grad.T


def solution(mesh):
    return jax.shard_map(
        shards,
        mesh=mesh,
        in_specs=(P("grp", None), P("grp", "vocab"), P("grp", "vocab"), P("grp"), P("grp")),
        out_specs=(P("grp"), P("grp", "vocab"), P("grp", "vocab")),
        check_vma=False,
    )
```

time: 592 us -> 165 us (0.28)
  waiting for transfers between devices: 301 us -> 0 us
  blocking collectives: 234 us -> 0 us
  Pallas kernels: 0 us -> 157 us
  matrix products: 17.5 us -> 0 us
  between operations: 15.2 us -> 1.29 us
  other arithmetic: 12.8 us -> 0 us
    reduce_scatter x2 -> x0, waiting for transfers between devices: 216 us -> none  [the longest x1 111 us: shards(): lax.psum_scatter(full_grad, 'vocab', scatter_dimension=1, tiled=True)]
    pallas_call x0 -> x1, Pallas kernels: none -> 157 us  [shards(): pl.pallas_call(functools.partial(fused_kernel, slab, chunks), name='disti...]
    psum x3 -> x0, blocking collectives: 126 us -> none  [the longest x1 53 us: shards(): divergence = lax.psum(jnp.sum(probs * log_ratio, axis=1), 'vocab')]
    all_gather x1 -> x0, waiting for transfers between devices: 85.3 us -> none  [shards(): piece = lax.all_gather(grad_logits, 'grp', axis=0, tiled=True)]
    pmax x1 -> x0, blocking collectives: 56.3 us -> none  [shards(): peak_s, peak_t = lax.pmax((local_peak_s, local_peak_t), 'vocab')]
    all_to_all x2 -> x0, blocking collectives: 51.6 us -> none  [the longest x1 29.4 us: shards(): lax.all_to_all(rows_part, 'grp', split_axis=0, concat_axis=1, tiled=True)]
    dot_general x3 -> x0, matrix products: 17.5 us -> none  [the longest x1 6.42 us: shards(): jnp.dot(block, weight, preferred_element_type=jnp.float32)]
  transfers between devices with their start and end apart: 4 -> 0, of which waited for: 3 -> 0; matrix products, arithmetic and copies ran while one was open for 2% -> 0% of each run, Pallas kernels for 0% -> 0%
where the time goes in v2:
time: 165 us; the launch traced here: 164 us
  Pallas kernels  157 us (95%)
  local copies, waits for them, and re-layouts  5.81 us (4%)
    pallas_call x1, Pallas kernels, shards(): pl.pallas_call(functools.partial(fused_kernel, slab, chunks), name='disti...  157 us
    unnamed x3, local copies, waits for them, and re-layouts  5.81 us

profile of v2, /device:TPU:6, one launch (start us, length us, event | category | flops | bytes accessed | tf_op | source)
XLA Modules:
  0.0 164.0 jit_solution(6129940209638751246)
XLA Ops:
  1.3 156.9 %distill.1 = (bf16[2374,512]{1,0:T(8,128)(2,1)}, bf16[128,128]{1,0:T(8,128)(2,1)}, f32[1,128]{1,0:T(1,128)}) custom-call(bf16[128,4096]{1,0:T(8,128)(2,1)} %hidden_ref.1, bf16[2374,512]{1,0:T(8,128)(2,1)} %bitcast.4, bf16[64,4748]{1,0:T(8,128)(2,1)} %panel_ref.1, s32[1,128]{1,0:T(1,128)} %bitcast.6, s32[1]{0:T(128)S(6)} %copy.11.count_ref), custom_call_target="tpu_custom_call" | custom-call | tf_op jit(solution)/shard_map/distill/pallas_call | solution.py:527
  158.2 1.2 copy.12
  159.3 1.4 copy.13
  160.7 3.3 %copy.14 = bf16[512,2374]{0,1:T(8,128)(2,1)} copy(bf16[512,2374]{0,1:T(8,128)(2,1)} %bitcast.5) | data formatting | bytes 4861952

commit v3 on v2

--- a/solution.py
+++ b/solution.py
@@ -12,7 +12,7 @@
 LOW = -1e30
 NX, NH, NYL, NZ, NC = 4, 2, 2, 8, 2
 TILE = 128
-GROUP_PEERS = [(dx, dh) for dh in (1, 0) for dx in (1, 3, 2, 0) if dx or dh]
+GROUP_PEERS = [(dx, dh) for dh in (1, 0) for dx in (0, 1, 3, 2) if dx or dh]
 PAIR_PEERS = [(dx, dc) for dc in (0, 1) for dx in (1, 3, 2, 0) if dx or dc]
 LINE_PEERS = [(dy, dz) for dy in (0, 1) for dz in range(NZ) if dy or dz]
 
@@ -73,20 +73,18 @@
     outcome,
     cols,
     every,
+    own,
     rows_out,
     paired,
     staged,
     lined,
     cross_out,
-    crossed,
-    final_out,
     final_in,
     local_sem,
     sent,
     got,
-    z_sent,
-    z_got,
-    end_sem,
+    end_sent,
+    end_got,
 ):
     x, h, yl, z, c = place()
     rows, depth = hidden_ref.shape[0], padded.shape[1]
@@ -97,12 +95,16 @@
     z_pair = z + 1 - 2 * lax.rem(z, 2)
     g = x * 2 + h
     v = yl * 16 + z * 2 + c
-    goal_g, goal_v = z, 4 * g + 2 * yl + c
-    from_g, from_v = v // 4, ((v % 4) // 2) * 16 + g * 2 + v % 2
-    moves = (goal_g != g) | (goal_v != v)
+    part = rows * NH // NZ
+    quarter = lax.rem(z, 4)
+    goals = {(p, b): (2 * p + z // 4, 4 * g + 2 * b + c) for p in range(NX) for b in range(NYL)}
+    origins = {
+        (b, k): (v // 4, b * 16 + ((g % 2) * 4 + k) * 2 + v % 2) for b in range(NYL) for k in range(4)
+    }
+    leaves = {key: (a != g) | (b != v) for key, (a, b) in goals.items()}
+    comes = {key: (a != g) | (b != v) for key, (a, b) in origins.items()}
     partner = device(x, 1 - h, yl, z, c)
     mate = device(x, h, yl, z, 1 - c)
-    across = device(x, h, 1 - yl, z, c)
     right, left = (x + 1) % NX, (x + NX - 1) % NX
     opposite = (x + 2) % NX
     to_right, to_left = device(right, h, yl, z, c), device(left, h, yl, z, c)
@@ -114,11 +116,13 @@
     for peer in peers:
         pl.semaphore_signal(barrier, inc=1, device_id=peer, device_id_type=MESH)
 
-    @pl.when(moves)
-    def _():
-        pl.semaphore_signal(
-            barrier, inc=1, device_id={"grp": from_g, "vocab": from_v}, device_id_type=MESH
-        )
+    for key, (a, b) in origins.items():
+
+        @pl.when(comes[key])
+        def _():
+            pl.semaphore_signal(
+                barrier, inc=1, device_id={"grp": a, "vocab": b}, device_id_type=MESH
+            )
 
     meta[...] = jnp.where(
         lax.broadcasted_iota(jnp.int32, meta.shape, 0) == 0,
@@ -128,7 +132,8 @@
     metas[g] = meta[...]
     padded[0:slab, :] = weight_ref[...]
     padded[slab:, :] = jnp.zeros((NX * width - slab, depth), padded.dtype)
-    pl.semaphore_wait(barrier, len(peers) + jnp.where(moves, 1, 0))
+    others = sum(jnp.where(leave, 1, 0) for leave in leaves.values())
+    pl.semaphore_wait(barrier, len(peers) + others)
 
     pending = []
 
@@ -212,6 +217,7 @@
 
     spread(above)
     spread_weight()
+    spread_weight()
     for dx, dh in GROUP_PEERS:
         met[dx, dh] = send(meta, metas.at[g], device((x + dx) % NX, (h + dh) % NH, yl, z, c))
     locals_ = [
@@ -232,8 +238,8 @@
     pass_on(above)
     spread_weight()
     pass_core(above)
+    spread(beside)
     spread_weight()
-    spread(beside)
     for copy in locals_:
         copy.wait()
     for peer in GROUP_PEERS:
@@ -354,6 +360,12 @@
         send(far.at[0], far.at[k + 1], device(x, h, (yl + dy) % NYL, (z + dz) % NZ, c))
         for k, (dy, dz) in enumerate(LINE_PEERS)
     ]
+    for side in range(NH):
+        for p in range(NX):
+            start, spot = side * half + p * rows, p * 2 * rows + side * rows
+            own[spot : spot + rows, :] = wide[
+                start : start + rows, pl.ds(pl.multiple_of(x * depth, depth), depth)
+            ]
     for k, slot in enumerate(slots):
         arrived(far.at[k + 1], slot)
     peak_s, sum_s, weighted, peak_t, sum_t, pick_s, pick_t = merge(far[...])
@@ -378,13 +390,14 @@
         outcome[:, k] = value
 
     def place_of(xs, hs, p, low=0, size=None):
-        start = pl.multiple_of(hs * half + p * rows + low, step)
+        start = pl.multiple_of(p * 2 * rows + hs * rows + low, step)
         return every.at[xs, pl.ds(start, rows if size is None else size), :]
 
-    own_start = h * half
+    per = rows // step
 
     def finish(i, carry):
         span = pl.ds(pl.multiple_of(i * step, step), step)
+        goal = pl.ds(pl.multiple_of((i // per * 2 + h) * rows + i % per * step, step), step)
         student = logits[span, :]
         raw = teach[span, :].astype(jnp.float32)
         table = cols[span, :]
@@ -393,7 +406,7 @@
         adv = table[:, 4:5]
         grad = probs * (table[:, 3:4] * ((student - raw) - table[:, 2:3]) + adv)
         grad = grad - jnp.where(chosen, adv, 0.0)
-        every[x, pl.ds(pl.multiple_of(own_start + i * step, step), step), :] = grad.astype(jnp.bfloat16)
+        every[x, goal, :] = grad.astype(jnp.bfloat16)
         return carry
 
     direct = []
@@ -403,7 +416,6 @@
             spot = place_of(x, h, len(direct))
             direct.append([send(spot, spot, to_right), send(spot, spot, to_left), send(spot, spot, partner)])
 
-    per = rows // step
     for p in range(NX):
         cols[p * rows : (p + 1) * rows, :] = to_columns(outcome[p])
         lax.fori_loop(p * per, (p + 1) * per, finish, 0)
@@ -411,32 +423,59 @@
             spread_grad()
 
     def rows_part(p):
+        start = p * 2 * rows
+        out = jnp.zeros((2 * rows, depth), jnp.float32)
+        for xs in range(NX):
+            out = out + jnp.dot(
+                every[xs, start : start + 2 * rows, :],
+                padded[xs * width : (xs + 1) * width, :],
+                preferred_element_type=jnp.float32,
+            )
         for side in range(NH):
-            start = side * half + p * rows
-            out = jnp.zeros((rows, depth), jnp.float32)
-            for xs in range(NX):
-                out = out + jnp.dot(
-                    every[xs, start : start + rows, :],
-                    padded[xs * width : (xs + 1) * width, :],
-                    preferred_element_type=jnp.float32,
-                )
             for s in range(4):
-                rows_out[p, s % 2, s // 2, side] = out[:, s * TILE : (s + 1) * TILE]
+                rows_out[p, s % 2, s // 2, side] = out[
+                    side * rows : (side + 1) * rows, s * TILE : (s + 1) * TILE
+                ]
         return send(rows_out.at[p, 1 - c], paired.at[p], mate)
+
+    lines = []
 
     def line_up(p, slot):
         arrived(paired.at[p], slot)
-        for side in range(NH):
-            t = 2 * p + side
+        for zt in range(NZ):
+            span = pl.ds(zt % 4 * part, part)
             for b in range(NYL):
-                staged[t, b] = rows_out[p, c, b, side] + paired[p, b, side]
-
-            @pl.when(z != t)
+                staged[p, zt, b] = rows_out[p, c, b, zt // 4, span, :] + paired[p, b, zt // 4, span, :]
+        lines.append(
+            [
+                send(
+                    staged.at[p, (z + dz) % NZ], lined.at[p, dz], device(x, h, yl, (z + dz) % NZ, c)
+                )
+                for dz in range(1, NZ)
+            ]
+        )
+
+    def deliver(p):
+        for dz in range(1, NZ):
+            arrived(lined.at[p, dz], lines[p][dz - 1])
+        total = staged[p, z]
+        for dz in range(1, NZ):
+            total = total + lined[p, dz]
+        cross_out[p] = total
+        span = pl.ds(pl.multiple_of(quarter * part, part), part)
+        for b in range(NYL):
+
+            @pl.when(leaves[p, b])
             def _():
                 pltpu.make_async_remote_copy(
-                    src_ref=staged.at[t], dst_ref=lined.at[z], send_sem=z_sent.at[t],
-                    recv_sem=z_got.at[z], device_id=device(x, h, yl, t, c), device_id_type=MESH,
+                    src_ref=cross_out.at[p, b], dst_ref=final_in.at[yl, span, :],
+                    send_sem=end_sent.at[p * NYL + b], recv_sem=end_got.at[yl * 4 + quarter],
+                    device_id={"grp": goals[p, b][0], "vocab": goals[p, b][1]}, device_id_type=MESH,
                 ).start()
+
+            @pl.when(jnp.logical_not(leaves[p, b]))
+            def _():
+                final_in[yl, span, :] = cross_out[p, b]
 
     far_own, last, paired_slots = [], [], []
     for p in range(NX + 3):
@@ -447,71 +486,68 @@
             arrived(place_of(right, h, p), direct[p][1])
             tail = place_of(right, h, p, step, step)
             far_own.append((a, send(tail, tail, to_left)))
-            spot = place_of(x, 1 - h, p)
-            arrived(spot, direct[p][2])
-            last.append([send(spot, spot, to_right), send(spot, spot, to_left)])
+            if p == NX - 1:
+                lower = place_of(left, h, p, step, step)
+                cross = [send(lower, lower, partner), send(tail, tail, partner)]
             spread_grad()
         if 1 <= p <= NX:
             q = p - 1
             arrived(place_of(opposite, h, q, 0, step), far_own[q][0])
             arrived(place_of(opposite, h, q, step, step), far_own[q][1])
             spot = place_of(opposite, h, q)
-            last[q].append(send(spot, spot, partner))
+            far_half = send(spot, spot, partner)
+            spot = place_of(x, 1 - h, q)
+            arrived(spot, direct[q][2])
+            if q == NX - 1:
+                spot = place_of(x, 1 - h, q, 0, step)
+            last.append([send(spot, spot, to_right), send(spot, spot, to_left), far_half])
+        if 3 <= p:
+            line_up(p - 3, paired_slots[p - 3])
         if 2 <= p <= NX + 1:
             q = p - 2
-            arrived(place_of(left, 1 - h, q), last[q][0])
-            arrived(place_of(right, 1 - h, q), last[q][1])
+            size = rows
+            if q == NX - 1:
+                size = step
+                arrived(place_of(left, 1 - h, q, step, step), cross[0])
+                arrived(place_of(right, 1 - h, q, step, step), cross[1])
+            arrived(place_of(left, 1 - h, q, 0, size), last[q][0])
+            arrived(place_of(right, 1 - h, q, 0, size), last[q][1])
             arrived(place_of(opposite, 1 - h, q), last[q][2])
             paired_slots.append(rows_part(q))
-        if 3 <= p:
-            line_up(p - 3, paired_slots[p - 3])
+    for p in range(NX - 2):
+        deliver(p)
 
     for xs in range(NX):
         size = min(width, slab - xs * width)
         out = lax.dot_general(
-            every[xs],
-            wide[:, pl.ds(pl.multiple_of(x * depth, depth), depth)],
-            (((0,), (0,)), ((), ())),
-            preferred_element_type=jnp.float32,
+            every[xs], own[...], (((0,), (0,)), ((), ())), preferred_element_type=jnp.float32
         )
         head_ref[xs * width : xs * width + size, :] = out[:size].astype(jnp.bfloat16)
-    lined[z] = staged[z]
-    for s in range(NZ):
-
-        @pl.when(z != s)
+    for p in (NX - 2, NX - 1):
+        deliver(p)
+    for b, k in origins:
+
+        @pl.when(comes[b, k])
         def _():
-            pltpu.make_async_copy(lined.at[s], lined.at[s], z_got.at[s]).wait()
-
-    total = lined[0]
-    for s in range(1, NZ):
-        total = total + lined[s]
-    staged[z] = total
-    cross_out[...] = staged[z, 1 - yl]
-    slot = send(cross_out, crossed, across)
-    arrived(crossed, slot)
-    final_out[...] = (staged[z, yl] + crossed[...]).astype(jnp.bfloat16)
-
-    @pl.when(moves)
-    def _():
-        copy = pltpu.make_async_remote_copy(
-            src_ref=final_out, dst_ref=final_in, send_sem=end_sem.at[0], recv_sem=end_sem.at[1],
-            device_id={"grp": goal_g, "vocab": goal_v}, device_id_type=MESH,
-        )
-        copy.start()
-        copy.wait()
-        out_ref[...] = final_in[...]
-
-    @pl.when(jnp.logical_not(moves))
-    def _():
-        out_ref[...] = final_out[...]
+            spot = final_in.at[b, pl.ds(k * part, part), :]
+            pltpu.make_async_copy(spot, spot, end_got.at[b * 4 + k]).wait()
+
+    out_ref[...] = (final_in[0] + final_in[1]).astype(jnp.bfloat16)
+    for p, b in goals:
+
+        @pl.when(leaves[p, b])
+        def _():
+            spot = cross_out.at[p, b]
+            pltpu.make_async_copy(spot, spot, end_sent.at[p * NYL + b]).wait()
 
     for copy in pending:
         copy.wait_send()
-    for t in range(NZ):
-
-        @pl.when(z != t)
-        def _():
-            pltpu.make_async_copy(staged.at[t], staged.at[t], z_sent.at[t]).wait()
+
+
+def write_kernel(*refs):
+    count = len(refs) // 2
+    for k in range(count):
+        refs[count + k][...] = refs[k][...]
 
 
 def shards(hidden, weight, teacher_panels, token_ids, row_counts):
@@ -521,9 +557,10 @@
     half, tokens = NX * rows, NX * NH * rows
     chunks = tuple((low, TILE) for low in range(0, width, TILE))
     m, q = len(PAIR_PEERS), len(LINE_PEERS)
+    part = rows * NH // NZ
     vmem = pl.BlockSpec(memory_space=pltpu.VMEM)
     f32, bf16 = jnp.float32, jnp.bfloat16
-    copies = 5 * len(GROUP_PEERS) + 4 * len(chunks) + 2 * m + q + 9 * NX + 1
+    copies = 5 * len(GROUP_PEERS) + 4 * len(chunks) + 2 * m + q + (9 + NZ - 1) * NX + 2
     head_grad, hidden_grad, kl = pl.pallas_call(
         functools.partial(fused_kernel, slab, chunks),
         name="distill",
@@ -550,25 +587,31 @@
             pltpu.VMEM((NX, 8, rows), f32),
             pltpu.VMEM((half, TILE), f32),
             pltpu.VMEM((NX, tokens, width), bf16),
+            pltpu.VMEM((tokens, depth), bf16),
             pltpu.VMEM((NX, NC, NYL, NH, rows, TILE), f32),
             pltpu.VMEM((NX, NYL, NH, rows, TILE), f32),
-            pltpu.VMEM((NZ, NYL, rows, TILE), f32),
-            pltpu.VMEM((NZ, NYL, rows, TILE), f32),
-            pltpu.VMEM((rows, TILE), f32),
-            pltpu.VMEM((rows, TILE), f32),
-            pltpu.VMEM((rows, TILE), bf16),
-            pltpu.VMEM((rows, TILE), bf16),
+            pltpu.VMEM((NX, NZ, NYL, part, TILE), f32),
+            pltpu.VMEM((NX, NZ, NYL, part, TILE), f32),
+            pltpu.VMEM((NX, NYL, part, TILE), f32),
+            pltpu.VMEM((NYL, rows, TILE), f32),
             pltpu.SemaphoreType.DMA((NX + 1,)),
             pltpu.SemaphoreType.DMA((copies,)),
             pltpu.SemaphoreType.DMA((copies,)),
-            pltpu.SemaphoreType.DMA((NZ,)),
-            pltpu.SemaphoreType.DMA((NZ,)),
-            pltpu.SemaphoreType.DMA((2,)),
+            pltpu.SemaphoreType.DMA((NX * NYL,)),
+            pltpu.SemaphoreType.DMA((NYL * 4,)),
         ],
         compiler_params=pltpu.CompilerParams(
             collective_id=1, has_side_effects=True, vmem_limit_bytes=56 * 2**20
         ),
     )(hidden, weight.T, teacher_panels, token_ids[None], row_counts)
+    results = (head_grad, hidden_grad, kl)
+    head_grad, hidden_grad, kl = pl.pallas_call(
+        write_kernel,
+        name="write",
+        out_shape=[jax.ShapeDtypeStruct(r.shape, r.dtype) for r in results],
+        in_specs=[vmem] * 3,
+        out_specs=[vmem] * 3,
+    )(*results)
     return kl[0], hidden_grad, head_grad.T
 
 

time: 165 us -> 157 us (0.952)
  local copies, waits for them, and re-layouts: 5.81 us -> 0 us
  Pallas kernels: 157 us -> 155 us
    unnamed x3 -> x0, local copies, waits for them, and re-layouts: 5.81 us -> none
    pallas_call x1, Pallas kernels: 157 us -> 152 us  [shards(): pl.pallas_call(functools.partial(fused_kernel, slab, chunks), name='disti...]
    pallas_call x0 -> x1, Pallas kernels: none -> 3.3 us  [shards(): pl.pallas_call(write_kernel, name='write', out_shape=[jax.ShapeDtypeStruc...]
where the time goes in v3:
time: 157 us; the launch traced here: 156 us
  Pallas kernels  155 us (99%)
    pallas_call x1, Pallas kernels, shards(): pl.pallas_call(functools.partial(fused_kernel, slab, chunks), name='disti...  152 us
    pallas_call x1, Pallas kernels, shards(): pl.pallas_call(write_kernel, name='write', out_shape=[jax.ShapeDtypeStruc...  3.3 us

profile of v3, /device:TPU:6, one launch (start us, length us, event | category | flops | bytes accessed | tf_op | source)
XLA Modules:
  0.0 156.4 jit_solution(8317897841776328043)
XLA Ops:
  1.3 151.8 %distill.1 = (bf16[2374,512]{1,0:T(8,128)(2,1)}, bf16[128,128]{1,0:T(8,128)(2,1)}, f32[1,128]{1,0:T(1,128)}) custom-call(bf16[128,4096]{1,0:T(8,128)(2,1)} %hidden_ref.1, bf16[2374,512]{1,0:T(8,128)(2,1)} %bitcast.4, bf16[64,4748]{1,0:T(8,128)(2,1)} %panel_ref.1, s32[1,128]{1,0:T(1,128)} %bitcast.5, s32[1]{0:T(128)S(6)} %copy.8.count_ref), custom_call_target="tpu_custom_call" | custom-call | tf_op jit(solution)/shard_map/distill/pallas_call | solution.py:564
  153.1 3.3 %write.1 = (bf16[2374,512]{1,0:T(8,128)(2,1)}, bf16[128,128]{1,0:T(8,128)(2,1)}, f32[1,128]{1,0:T(1,128)}) custom-call(bf16[2374,512]{1,0:T(8,128)(2,1)} %get-tuple-element.9.refs_0_, bf16[128,128]{1,0:T(8,128)(2,1)} %get-tuple-element.10.refs_1_, f32[1,128]{1,0:T(1,128)} %get-tuple-element.11.refs_2_), custom_call_target="tpu_custom_call" | custom-call | tf_op jit(solution)/shard_map/write/pallas_call | solution.py:608

commit v4 on v3

--- a/solution.py
+++ b/solution.py
@@ -50,14 +50,17 @@
 def fused_kernel(
     slab,
     chunks,
+    hidden_hbm,
+    weight_hbm,
+    panel_hbm,
+    token_ref,
+    count_ref,
+    head_hbm,
+    out_ref,
+    kl_ref,
     hidden_ref,
     weight_ref,
     panel_ref,
-    token_ref,
-    count_ref,
-    head_ref,
-    out_ref,
-    kl_ref,
     padded,
     wide,
     heads,
@@ -70,6 +73,7 @@
     metas,
     near,
     far,
+    merged,
     outcome,
     cols,
     every,
@@ -109,6 +113,13 @@
     opposite = (x + 2) % NX
     to_right, to_left = device(right, h, yl, z, c), device(left, h, yl, z, c)
 
+    loads = [
+        pltpu.make_async_copy(hidden_hbm, hidden_ref, local_sem.at[NX + 1]),
+        pltpu.make_async_copy(weight_hbm, weight_ref, local_sem.at[NX + 2]),
+        pltpu.make_async_copy(panel_hbm, panel_ref, local_sem.at[NX + 3]),
+    ]
+    for load in loads:
+        load.start()
     barrier = pltpu.get_barrier_semaphore()
     peers = [device((x + dx) % NX, (h + dh) % NH, yl, z, c) for dx, dh in GROUP_PEERS]
     peers += [device((x + dx) % NX, h, yl, z, 1 - c) for dx in range(NX)]
@@ -130,6 +141,8 @@
         count_ref[0].astype(jnp.float32),
     )
     metas[g] = meta[...]
+    loads[0].wait()
+    loads[1].wait()
     padded[0:slab, :] = weight_ref[...]
     padded[slab:, :] = jnp.zeros((NX * width - slab, depth), padded.dtype)
     others = sum(jnp.where(leave, 1, 0) for leave in leaves.values())
@@ -231,6 +244,7 @@
     for copy in locals_:
         copy.start()
 
+    loads[2].wait()
     teacher[...] = jnp.zeros_like(teacher)
     for side in range(NC):
         teacher[side, :, 0:slab] = panel_ref[:, side * slab : (side + 1) * slab]
@@ -353,13 +367,14 @@
     for k, slot in enumerate(slots):
         arrived(near.at[k + 1], slot)
     for k, value in enumerate(merge(near[:, :, 1:8])):
-        far[0, :, k] = value
-    token_row = near[0, :, 0]
-    far[0, :, 7] = token_row
+        merged[:, k] = value
+    merged[:, 7] = near[0, :, 0]
+    pair = pl.ds(2 * c, 2)
     slots = [
-        send(far.at[0], far.at[k + 1], device(x, h, (yl + dy) % NYL, (z + dz) % NZ, c))
+        send(merged.at[pair], far.at[k + 1], device(x, h, (yl + dy) % NYL, (z + dz) % NZ, c))
         for k, (dy, dz) in enumerate(LINE_PEERS)
     ]
+    far[0] = merged[pair]
     for side in range(NH):
         for p in range(NX):
             start, spot = side * half + p * rows, p * 2 * rows + side * rows
@@ -376,18 +391,19 @@
     mean_gap = weighted / sum_s
     divergence = mean_gap - student_norm + teacher_norm
     advantage = (pick_t - teacher_norm) - (pick_s - student_norm)
-    counts = jnp.stack([metas[group * 2 + h][1] for group in range(NX)], axis=0)
-    valid = lax.broadcasted_iota(jnp.int32, (NX, rows), 1).astype(jnp.float32) < counts
+    counts = jnp.stack([metas[(2 * c + k) * 2 + h][1] for k in range(2)], axis=0)
+    valid = lax.broadcasted_iota(jnp.int32, (2, rows), 1).astype(jnp.float32) < counts
     row_weight = jnp.where(valid, rows / total_rows, 0.0)
     kl = jnp.where(valid, divergence, 0.0)
-    own_group = lax.broadcasted_iota(jnp.int32, (NX, rows), 0) == x
-    kl_ref[...] = jnp.sum(jnp.where(own_group, kl, 0.0), axis=0, keepdims=True)
+    token_row = far[0, :, 7]
     table = [
-        peak_s, 1.0 / sum_s, mean_gap, row_weight * KL_SCALE, row_weight * advantage, token_row,
-        token_row, token_row,
+        peak_s, 1.0 / sum_s, mean_gap, row_weight * KL_SCALE, row_weight * advantage, token_row, kl, kl,
     ]
     for k, value in enumerate(table):
-        outcome[:, k] = value
+        outcome[pair, k] = value
+    slot = send(outcome.at[pair], outcome.at[pair], mate)
+    arrived(outcome.at[pl.ds(2 - 2 * c, 2)], slot)
+    kl_ref[...] = outcome[x, 6:7]
 
     def place_of(xs, hs, p, low=0, size=None):
         start = pl.multiple_of(p * 2 * rows + hs * rows + low, step)
@@ -522,7 +538,9 @@
         out = lax.dot_general(
             every[xs], own[...], (((0,), (0,)), ((), ())), preferred_element_type=jnp.float32
         )
-        head_ref[xs * width : xs * width + size, :] = out[:size].astype(jnp.bfloat16)
+        weight_ref[xs * width : xs * width + size, :] = out[:size].astype(jnp.bfloat16)
+    store = pltpu.make_async_copy(weight_ref, head_hbm, local_sem.at[NX + 2])
+    store.start()
     for p in (NX - 2, NX - 1):
         deliver(p)
     for b, k in origins:
@@ -542,6 +560,7 @@
 
     for copy in pending:
         copy.wait_send()
+    store.wait()
 
 
 def write_kernel(*refs):
@@ -559,8 +578,9 @@
     m, q = len(PAIR_PEERS), len(LINE_PEERS)
     part = rows * NH // NZ
     vmem = pl.BlockSpec(memory_space=pltpu.VMEM)
+    hbm = pl.BlockSpec(memory_space=pl.ANY)
     f32, bf16 = jnp.float32, jnp.bfloat16
-    copies = 5 * len(GROUP_PEERS) + 4 * len(chunks) + 2 * m + q + (9 + NZ - 1) * NX + 2
+    copies = 5 * len(GROUP_PEERS) + 4 * len(chunks) + 2 * m + q + (9 + NZ - 1) * NX + 3
     head_grad, hidden_grad, kl = pl.pallas_call(
         functools.partial(fused_kernel, slab, chunks),
         name="distill",
@@ -569,9 +589,12 @@
             jax.ShapeDtypeStruct((rows, TILE), bf16),
             jax.ShapeDtypeStruct((1, rows), f32),
         ],
-        in_specs=[vmem] * 4 + [pl.BlockSpec(memory_space=pltpu.SMEM)],
-        out_specs=[vmem] * 3,
+        in_specs=[hbm] * 3 + [vmem, pl.BlockSpec(memory_space=pltpu.SMEM)],
+        out_specs=[hbm, vmem, vmem],
         scratch_shapes=[
+            pltpu.VMEM(hidden.shape, bf16),
+            pltpu.VMEM((slab, depth), bf16),
+            pltpu.VMEM(teacher_panels.shape, bf16),
             pltpu.VMEM((NX * width, depth), bf16),
             pltpu.VMEM((tokens, NX * depth), bf16),
             pltpu.VMEM((width, NX * depth), bf16),
@@ -583,7 +606,8 @@
             pltpu.VMEM((8, rows), f32),
             pltpu.VMEM((NX * NH, 8, rows), f32),
             pltpu.VMEM((m + 1, NX, 8, rows), f32),
-            pltpu.VMEM((q + 1, NX, 8, rows), f32),
+            pltpu.VMEM((q + 1, 2, 8, rows), f32),
+            pltpu.VMEM((NX, 8, rows), f32),
             pltpu.VMEM((NX, 8, rows), f32),
             pltpu.VMEM((half, TILE), f32),
             pltpu.VMEM((NX, tokens, width), bf16),
@@ -594,7 +618,7 @@
             pltpu.VMEM((NX, NZ, NYL, part, TILE), f32),
             pltpu.VMEM((NX, NYL, part, TILE), f32),
             pltpu.VMEM((NYL, rows, TILE), f32),
-            pltpu.SemaphoreType.DMA((NX + 1,)),
+            pltpu.SemaphoreType.DMA((NX + 4,)),
             pltpu.SemaphoreType.DMA((copies,)),
             pltpu.SemaphoreType.DMA((copies,)),
             pltpu.SemaphoreType.DMA((NX * NYL,)),

time: 157 us -> 153 us (0.975)
  Pallas kernels: 155 us -> 152 us
    pallas_call x1, Pallas kernels: 152 us -> 149 us  [shards(): pl.pallas_call(functools.partial(fused_kernel, slab, chunks), name='disti...]
where the time goes in v4:
time: 153 us
  Pallas kernels  152 us (99%)
    pallas_call x1, Pallas kernels, shards(): pl.pallas_call(functools.partial(fused_kernel, slab, chunks), name='disti...  149 us
    pallas_call x1, Pallas kernels, shards(): pl.pallas_call(write_kernel, name='write', out_shape=[jax.ShapeDtypeStruc...  3.3 us

profile of v4, /device:TPU:6, one launch (start us, length us, event | category | flops | bytes accessed | tf_op | source)
XLA Modules:
  0.0 153.2 jit_solution(11218755215815092072)
XLA Ops:
  1.3 148.6 %distill.1 = (bf16[2374,512]{1,0:T(8,128)(2,1)}, bf16[128,128]{1,0:T(8,128)(2,1)}, f32[1,128]{1,0:T(1,128)}) custom-call(bf16[128,4096]{1,0:T(8,128)(2,1)} %hidden_hbm.1, bf16[2374,512]{1,0:T(8,128)(2,1)} %bitcast.4, bf16[64,4748]{1,0:T(8,128)(2,1)} %panel_hbm.1, s32[1,128]{1,0:T(1,128)} %bitcast.5, s32[1]{0:T(128)S(6)} %copy.8.count_ref), custom_call_target="tpu_custom_call" | custom-call | tf_op jit(solution)/shard_map/distill/pallas_call | solution.py:584
  149.9 3.3 %write.1 = (bf16[2374,512]{1,0:T(8,128)(2,1)}, bf16[128,128]{1,0:T(8,128)(2,1)}, f32[1,128]{1,0:T(1,128)}) custom-call(bf16[2374,512]{1,0:T(8,128)(2,1)} %get-tuple-element.9.refs_0_, bf16[128,128]{1,0:T(8,128)(2,1)} %get-tuple-element.10.refs_1_, f32[1,128]{1,0:T(1,128)} %get-tuple-element.11.refs_2_), custom_call_target="tpu_custom_call" | custom-call | tf_op jit(solution)/shard_map/write/pallas_call | solution.py:632

commit v5 on v4

--- a/solution.py
+++ b/solution.py
@@ -53,13 +53,14 @@
     hidden_hbm,
     weight_hbm,
     panel_hbm,
+    tail_ref,
     token_ref,
     count_ref,
     head_hbm,
     out_ref,
     kl_ref,
     hidden_ref,
-    weight_ref,
+    head_ref,
     panel_ref,
     padded,
     wide,
@@ -113,9 +114,12 @@
     opposite = (x + 2) % NX
     to_right, to_left = device(right, h, yl, z, c), device(left, h, yl, z, c)
 
+    whole = slab // 16 * 16
     loads = [
         pltpu.make_async_copy(hidden_hbm, hidden_ref, local_sem.at[NX + 1]),
-        pltpu.make_async_copy(weight_hbm, weight_ref, local_sem.at[NX + 2]),
+        pltpu.make_async_copy(
+            weight_hbm.at[pl.ds(0, whole)], padded.at[pl.ds(0, whole)], local_sem.at[NX + 2]
+        ),
         pltpu.make_async_copy(panel_hbm, panel_ref, local_sem.at[NX + 3]),
     ]
     for load in loads:
@@ -141,10 +145,10 @@
         count_ref[0].astype(jnp.float32),
     )
     metas[g] = meta[...]
+    padded[whole : whole + 16, :] = tail_ref[...]
+    padded[whole + 16 :, :] = jnp.zeros((NX * width - whole - 16, depth), padded.dtype)
     loads[0].wait()
     loads[1].wait()
-    padded[0:slab, :] = weight_ref[...]
-    padded[slab:, :] = jnp.zeros((NX * width - slab, depth), padded.dtype)
     others = sum(jnp.where(leave, 1, 0) for leave in leaves.values())
     pl.semaphore_wait(barrier, len(peers) + others)
 
@@ -534,12 +538,11 @@
         deliver(p)
 
     for xs in range(NX):
-        size = min(width, slab - xs * width)
         out = lax.dot_general(
             every[xs], own[...], (((0,), (0,)), ((), ())), preferred_element_type=jnp.float32
         )
-        weight_ref[xs * width : xs * width + size, :] = out[:size].astype(jnp.bfloat16)
-    store = pltpu.make_async_copy(weight_ref, head_hbm, local_sem.at[NX + 2])
+        head_ref[xs * width : (xs + 1) * width, :] = out.astype(jnp.bfloat16)
+    store = pltpu.make_async_copy(head_ref, head_hbm, local_sem.at[NX + 2])
     store.start()
     for p in (NX - 2, NX - 1):
         deliver(p)
@@ -561,12 +564,6 @@
     for copy in pending:
         copy.wait_send()
     store.wait()
-
-
-def write_kernel(*refs):
-    count = len(refs) // 2
-    for k in range(count):
-        refs[count + k][...] = refs[k][...]
 
 
 def shards(hidden, weight, teacher_panels, token_ids, row_counts):
@@ -575,6 +572,9 @@
     width = -(-slab // (NX * TILE)) * TILE
     half, tokens = NX * rows, NX * NH * rows
     chunks = tuple((low, TILE) for low in range(0, width, TILE))
+    turned = weight.T
+    whole = slab // 16 * 16
+    tail = jnp.pad(turned[whole:], ((0, 16 - (slab - whole)), (0, 0)))
     m, q = len(PAIR_PEERS), len(LINE_PEERS)
     part = rows * NH // NZ
     vmem = pl.BlockSpec(memory_space=pltpu.VMEM)
@@ -585,15 +585,15 @@
         functools.partial(fused_kernel, slab, chunks),
         name="distill",
         out_shape=[
-            jax.ShapeDtypeStruct((slab, depth), bf16),
+            jax.ShapeDtypeStruct((NX * width, depth), bf16),
             jax.ShapeDtypeStruct((rows, TILE), bf16),
             jax.ShapeDtypeStruct((1, rows), f32),
         ],
-        in_specs=[hbm] * 3 + [vmem, pl.BlockSpec(memory_space=pltpu.SMEM)],
+        in_specs=[hbm] * 3 + [vmem] * 2 + [pl.BlockSpec(memory_space=pltpu.SMEM)],
         out_specs=[hbm, vmem, vmem],
         scratch_shapes=[
             pltpu.VMEM(hidden.shape, bf16),
-            pltpu.VMEM((slab, depth), bf16),
+            pltpu.VMEM((NX * width, depth), bf16),
             pltpu.VMEM(teacher_panels.shape, bf16),
             pltpu.VMEM((NX * width, depth), bf16),
             pltpu.VMEM((tokens, NX * depth), bf16),
@@ -627,16 +627,8 @@
         compiler_params=pltpu.CompilerParams(
             collective_id=1, has_side_effects=True, vmem_limit_bytes=56 * 2**20
         ),
-    )(hidden, weight.T, teacher_panels, token_ids[None], row_counts)
-    results = (head_grad, hidden_grad, kl)
-    head_grad, hidden_grad, kl = pl.pallas_call(
-        write_kernel,
-        name="write",
-        out_shape=[jax.ShapeDtypeStruct(r.shape, r.dtype) for r in results],
-        in_specs=[vmem] * 3,
-        out_specs=[vmem] * 3,
-    )(*results)
-    return kl[0], hidden_grad, head_grad.T
+    )(hidden, turned, teacher_panels, tail, token_ids[None], row_counts)
+    return kl[0], hidden_grad, head_grad[:slab].T
 
 
 def solution(mesh):

time: 153 us -> 156 us (1.020)
  local copies, waits for them, and re-layouts: 0 us -> 5.73 us
  Pallas kernels: 152 us -> 149 us
    pallas_call x1 -> x0, Pallas kernels: 3.3 us -> none  [shards(): pl.pallas_call(write_kernel, name='write', out_shape=[jax.ShapeDtypeStruc...]
    transpose x0 -> x1, local copies, waits for them, and re-layouts: none -> 3.28 us  [shards(): return (kl[0], hidden_grad, head_grad[:slab].T)]
where the time goes in v5:
time: 156 us
  Pallas kernels  149 us (96%)
  local copies, waits for them, and re-layouts  5.73 us (4%)
    pallas_call x1, Pallas kernels, shards(): pl.pallas_call(functools.partial(fused_kernel, slab, chunks), name='disti...  149 us
    transpose x1, local copies, waits for them, and re-layouts, shards(): return (kl[0], hidden_grad, head_grad[:slab].T)  3.28 us

profile of v5, /device:TPU:6, one launch (start us, length us, event | category | flops | bytes accessed | tf_op | source)
XLA Modules:
  0.0 155.6 jit_solution(7199658671332073513)
XLA Ops:
  1.3 0.7 slice.8
  2.0 0.6 pad.4.tail_ref
  2.6 148.5 %distill.1 = (bf16[2560,512]{1,0:T(8,128)(2,1)}, bf16[128,128]{1,0:T(8,128)(2,1)}, f32[1,128]{1,0:T(1,128)}) custom-call(bf16[128,4096]{1,0:T(8,128)(2,1)} %hidden_hbm.1, bf16[2374,512]{1,0:T(8,128)(2,1)} %bitcast.6, bf16[64,4748]{1,0:T(8,128)(2,1)} %panel_hbm.1, bf16[16,512]{1,0:T(8,128)(2,1)} %pad.4.tail_ref, s32[1,128]{1,0:T(1,128)} %bitcast.7, ...), custom_call_target="tpu_custom_call" | custom-call | tf_op jit(solution)/shard_map/distill/pallas_call | solution.py:584
  151.1 0.0 copy-start.1
  151.1 0.0 copy-start
  151.1 3.3 %slice_bitcast_fusion = bf16[512,2374]{0,1:T(8,128)(2,1)} fusion(bf16[2560,512]{1,0:T(8,128)(2,1)} %get-tuple-element.8), kind=kLoop, calls=%fused_computation | loop fusion | bytes 4861952 | tf_op jit(solution)/shard_map/transpose | solution.py:631
  154.4 0.0 copy-done.1
  154.4 0.5 copy.11
  154.9 0.0 copy-done
  154.9 0.6 copy.12
Async XLA Ops:
  151.1 3.3 %copy-start.1 = (f32[1,128]{1,0:T(1,128)S(1)}, f32[1,128]{1,0:T(1,128)}, u32[]{:S(2)}) copy-start(f32[1,128]{1,0:T(1,128)} %get-tuple-element.6) | copy-start | bytes 1540
  151.1 3.8 %copy-start = (bf16[128,128]{1,0:T(8,128)(2,1)S(1)}, bf16[128,128]{1,0:T(8,128)(2,1)}, u32[]{:S(2)}) copy-start(bf16[128,128]{1,0:T(8,128)(2,1)} %get-tuple-element.13) | copy-start | bytes 98308

commit v6 on v5

--- a/solution.py
+++ b/solution.py
@@ -235,6 +235,7 @@
     spread(above)
     spread_weight()
     spread_weight()
+    spread_weight()
     for dx, dh in GROUP_PEERS:
         met[dx, dh] = send(meta, metas.at[g], device((x + dx) % NX, (h + dh) % NH, yl, z, c))
     locals_ = [

time: 156 us -> 155 us (level)
  no operation moved by 1% of the time
where the time goes in v6:
time: 155 us
  Pallas kernels  148 us (95%)
  local copies, waits for them, and re-layouts  5.73 us (4%)
    pallas_call x1, Pallas kernels, shards(): pl.pallas_call(functools.partial(fused_kernel, slab, chunks), name='disti...  148 us
    transpose x1, local copies, waits for them, and re-layouts, shards(): return (kl[0], hidden_grad, head_grad[:slab].T)  3.28 us

profile of v6, /device:TPU:6, one launch (start us, length us, event | category | flops | bytes accessed | tf_op | source)
XLA Modules:
  0.0 154.9 jit_solution(4097697564500332159)
XLA Ops:
  1.3 0.7 slice.8
  2.0 0.6 pad.4.tail_ref
  2.6 147.9 %distill.1 = (bf16[2560,512]{1,0:T(8,128)(2,1)}, bf16[128,128]{1,0:T(8,128)(2,1)}, f32[1,128]{1,0:T(1,128)}) custom-call(bf16[128,4096]{1,0:T(8,128)(2,1)} %hidden_hbm.1, bf16[2374,512]{1,0:T(8,128)(2,1)} %bitcast.6, bf16[64,4748]{1,0:T(8,128)(2,1)} %panel_hbm.1, bf16[16,512]{1,0:T(8,128)(2,1)} %pad.4.tail_ref, s32[1,128]{1,0:T(1,128)} %bitcast.7, ...), custom_call_target="tpu_custom_call" | custom-call | tf_op jit(solution)/shard_map/distill/pallas_call | solution.py:585
  150.5 0.0 copy-start.1
  150.5 0.0 copy-start
  150.5 3.3 %slice_bitcast_fusion = bf16[512,2374]{0,1:T(8,128)(2,1)} fusion(bf16[2560,512]{1,0:T(8,128)(2,1)} %get-tuple-element.8), kind=kLoop, calls=%fused_computation | loop fusion | bytes 4861952 | tf_op jit(solution)/shard_map/transpose | solution.py:632
  153.8 0.0 copy-done.1
  153.8 0.5 copy.11
  154.3 0.0 copy-done
  154.3 0.6 copy.12
Async XLA Ops:
  150.5 3.3 %copy-start.1 = (f32[1,128]{1,0:T(1,128)S(1)}, f32[1,128]{1,0:T(1,128)}, u32[]{:S(2)}) copy-start(f32[1,128]{1,0:T(1,128)} %get-tuple-element.6) | copy-start | bytes 1540
  150.5 3.8 %copy-start = (bf16[128,128]{1,0:T(8,128)(2,1)S(1)}, bf16[128,128]{1,0:T(8,128)(2,1)}, u32[]{:S(2)}) copy-start(bf16[128,128]{1,0:T(8,128)(2,1)} %get-tuple-element.13) | copy-start | bytes 98308
